TPU v7x, 128 devices: a whole 4x4x4 slice. The times are simulated.
128 devices in a mesh: grp: 4 (over x_hi, core), fsdp: 32 (over y, z, x_lo).
Axes of the slice: x: 4 (x_hi: 2, x_lo: 2; x = x_hi * 2 + x_lo), y: 4, z: 4, core: 2. Of those that a mesh axis runs over, the one named last changes fastest.
Arguments:
- caption_states: bfloat16 [32, 128, 4096], P('fsdp'), may hold values from -6 to 6
- caption_lens: int32 [32], replicated, may hold values from 4 to 128
- text_gain: float32 [4096], replicated, may hold values from 0.25 to 1.75
- text_query: bfloat16 [4096, 2048], P(None, 'grp'), may hold values from -0.01171875 to 0.01171875
- text_key: bfloat16 [4096, 2048], P(None, 'grp'), may hold values from -0.09375 to 0.09375
- text_value: bfloat16 [4096, 2048], P(None, 'grp'), may hold values from -0.09375 to 0.09375
- text_bias: float32 [32, 128, 128], P('grp'), may hold values from -4 to 4
- text_out: bfloat16 [2048, 4096], P('grp'), may hold values from -0.125 to 0.125
- final_gain: float32 [4096], replicated, may hold values from 0.25 to 1.75
- cross_key: bfloat16 [4096, 1536], P('fsdp', 'grp'), may hold values from -0.09375 to 0.09375
- cross_value: bfloat16 [4096, 1536], P('fsdp', 'grp'), may hold values from -0.09375 to 0.09375
- video_states: bfloat16 [8192, 3072], P('fsdp'), may hold values from -6 to 6
- video_counts: int32 [32], replicated, may hold values from 128 to 1024, as said below
- sample_caption: int32 [32], replicated, may hold values from 0 to 31, each once
- cross_query: bfloat16 [3072, 1536], P('fsdp', 'grp'), may hold values from -0.109375 to 0.109375
- cross_out: bfloat16 [1536, 3072], P('grp', 'fsdp'), may hold values from -0.15625 to 0.15625
- out_grad: bfloat16 [8192, 3072], P('fsdp'), may hold values from -6 to 6
Outputs:
- updated: bfloat16 [8192, 3072], P('fsdp', 'grp')
- input_grad: bfloat16 [8192, 3072], P('fsdp', 'grp')
- query_grad: float32 [3072, 1536], P('fsdp', 'grp')
- out_weight_grad: float32 [1536, 3072], P('grp', 'fsdp')
- key_grad: bfloat16 [32, 128, 1536], P('fsdp', None, 'grp')
- value_grad: bfloat16 [32, 128, 1536], P('fsdp', None, 'grp')
Inputs may be any that keep to these rules, and one draw needn't show every extreme that they name: `video_counts`: counts of the samples in order, summing to 8192. `sample_caption`: each caption belongs to exactly one sample.
All inputs are finite; a program needn't handle non-finite values.
Results may differ from a plain program's by a relative error of at most 0.04.
Values may be sent and summed in bfloat16 or wider, within the bound.
A program may use at most 128 MiB of HBM per device.

v0:
```python
import math

import jax
import jax.numpy as jnp
from jax import lax
from jax.sharding import PartitionSpec as P

HEAD_SIZE = 128


def rms_scale(values, gain):
    mean_square = jnp.mean(values * values, axis=-1, keepdims=True)
    return values * lax.rsqrt(mean_square + 1e-06) * gain


def contract_last(left, right):
    return lax.dot_general(
        left, right, (((1,), (1,)), ((), ())), preferred_element_type=jnp.float32
    )


def contract_first(left, right):
    return lax.dot_general(
        left, right, (((0,), (0,)), ((), ())), preferred_element_type=jnp.float32
    )


def local(
    caption_states,
    caption_lens,
    text_gain,
    text_query,
    text_key,
    text_value,
    text_bias,
    text_out,
    final_gain,
    cross_key,
    cross_value,
    video_states,
    video_counts,
    sample_caption,
    cross_query,
    cross_out,
    out_grad,
):
    column = lax.axis_index("fsdp")
    caps_local, cap_len, text_width = caption_states.shape
    local_lens = lax.dynamic_slice_in_dim(caption_lens, column * caps_local, caps_local)
    flat_states = caption_states.reshape(caps_local * cap_len, text_width).astype(jnp.float32)
    text_normed = rms_scale(flat_states, text_gain).astype(jnp.bfloat16)
    local_heads = text_bias.shape[0]
    head_width = text_query.shape[1] // local_heads

    def heads_of(weight):
        product = jnp.dot(text_normed, weight, preferred_element_type=jnp.float32).astype(
            jnp.bfloat16
        )
        return product.reshape(caps_local, cap_len, local_heads, head_width)

    text_queries = heads_of(text_query)
    text_keys = heads_of(text_key)
    text_values = heads_of(text_value)
    text_scores = (
        jnp.einsum("cihd,cjhd->chij", text_queries, text_keys, preferred_element_type=jnp.float32)
        + text_bias[None]
    )
    key_valid = jnp.arange(cap_len, dtype=jnp.int32)[None, :] < local_lens[:, None]
    exp_scores = jnp.where(key_valid[:, None, None, :], jnp.exp(text_scores), 0.0)
    text_weights = (exp_scores / jnp.sum(exp_scores, axis=-1, keepdims=True)).astype(jnp.bfloat16)
    text_mixed = jnp.einsum(
        "chij,cjhd->cihd", text_weights, text_values, preferred_element_type=jnp.float32
    )
    text_mixed = text_mixed.astype(jnp.bfloat16).reshape(
        caps_local * cap_len, local_heads * head_width
    )
    partial_value = jnp.dot(text_mixed, text_out, preferred_element_type=jnp.float32)
    summed = lax.psum(partial_value.astype(jnp.bfloat16), "grp").astype(jnp.float32)
    encoded = rms_scale(flat_states + summed, final_gain).astype(jnp.bfloat16)
    width_local = cross_key.shape[1]
    columns_in = encoded
    key_sum = jnp.dot(
        columns_in,
        lax.all_gather(cross_key, "fsdp", axis=0, tiled=True),
        preferred_element_type=jnp.float32,
    )
    value_sum = jnp.dot(
        columns_in,
        lax.all_gather(cross_value, "fsdp", axis=0, tiled=True),
        preferred_element_type=jnp.float32,
    )
    cap_keys = key_sum.astype(jnp.bfloat16).reshape(caps_local, cap_len, width_local)
    cap_values = value_sum.astype(jnp.bfloat16).reshape(caps_local, cap_len, width_local)
    all_keys, all_values = (
        lax.all_gather(cap_keys, "fsdp", axis=0, tiled=True),
        lax.all_gather(cap_values, "fsdp", axis=0, tiled=True),
    )
    caption_total = all_keys.shape[0]
    tokens, model_width = video_states.shape
    positions = column * tokens + jnp.arange(tokens, dtype=jnp.int32)
    sample_end = jnp.cumsum(video_counts)
    token_sample = jnp.sum((sample_end[None, :] <= positions[:, None]).astype(jnp.int32), axis=1)
    slot_count = 3
    slot_sample = token_sample[0] + jnp.arange(slot_count, dtype=jnp.int32)
    slot_valid = slot_sample < caption_total
    slot_clipped = jnp.minimum(slot_sample, caption_total - 1)
    numbers = jnp.arange(caption_total, dtype=jnp.int32)
    slot_pick = slot_clipped[:, None] == numbers[None, :]
    slot_caption = jnp.sum(jnp.where(slot_pick, sample_caption[None, :], 0), axis=1)
    caption_pick = slot_caption[:, None] == numbers[None, :]
    slot_lens = jnp.sum(jnp.where(caption_pick, caption_lens[None, :], 0), axis=1)
    slot_member = token_sample[None, :] == slot_sample[:, None]
    member_float = slot_member.astype(jnp.float32)
    member_half = slot_member.astype(jnp.bfloat16)
    cross_local = width_local // HEAD_SIZE
    slot_keys = jnp.take(all_keys, slot_caption, axis=0).reshape(
        slot_count, cap_len, cross_local, HEAD_SIZE
    )
    slot_values = jnp.take(all_values, slot_caption, axis=0).reshape(
        slot_count, cap_len, cross_local, HEAD_SIZE
    )
    token_lens = jnp.sum(jnp.where(slot_member, slot_lens[:, None], 0), axis=0)
    video = video_states.astype(jnp.float32)
    center = video - jnp.mean(video, axis=-1, keepdims=True)
    inverse = lax.rsqrt(jnp.mean(center * center, axis=-1, keepdims=True) + 1e-06)
    video_hat = center * inverse
    video_normed = video_hat.astype(jnp.bfloat16)
    columns_in = video_normed
    queries = jnp.dot(
        columns_in,
        lax.all_gather(cross_query, "fsdp", axis=0, tiled=True),
        preferred_element_type=jnp.float32,
    ).astype(jnp.bfloat16)
    score_scale = 1.0 / math.sqrt(HEAD_SIZE)
    query_heads = queries.reshape(tokens, cross_local, HEAD_SIZE)
    slot_scores = jnp.einsum(
        "thd,kjhd->kthj", query_heads, slot_keys, preferred_element_type=jnp.float32
    )
    scores = jnp.sum(member_float[:, :, None, None] * slot_scores, axis=0) * score_scale
    token_valid = (jnp.arange(cap_len, dtype=jnp.int32)[None, :] < token_lens[:, None])[:, None, :]
    exp_video = jnp.where(token_valid, jnp.exp(scores), 0.0)
    weights = exp_video / jnp.sum(exp_video, axis=-1, keepdims=True)
    probs = weights.astype(jnp.bfloat16)
    masked_probs = member_half[:, :, None, None] * probs[None]
    attended = jnp.einsum(
        "kthj,kjhd->thd", masked_probs, slot_values, preferred_element_type=jnp.float32
    )
    attended = attended.astype(jnp.bfloat16).reshape(tokens, width_local)
    partial_out = jnp.dot(
        attended,
        lax.all_gather(cross_out, "fsdp", axis=1, tiled=True),
        preferred_element_type=jnp.float32,
    )
    out_share = lax.psum_scatter(
        partial_out.astype(jnp.bfloat16), "grp", scatter_dimension=1, tiled=True
    ).astype(jnp.float32)
    slice_width = out_share.shape[1]
    feature_start = lax.axis_index("grp") * slice_width
    updated = (lax.dynamic_slice_in_dim(video, feature_start, slice_width, 1) + out_share).astype(
        jnp.bfloat16
    )
    d_attended = contract_last(out_grad, lax.all_gather(cross_out, "fsdp", axis=1, tiled=True))
    d_attended = d_attended.astype(jnp.bfloat16).reshape(tokens, cross_local, HEAD_SIZE)
    slot_dprobs = jnp.einsum(
        "thd,kjhd->kthj", d_attended, slot_values, preferred_element_type=jnp.float32
    )
    d_probs = jnp.sum(member_float[:, :, None, None] * slot_dprobs, axis=0)
    d_scores = (
        weights * (d_probs - jnp.sum(weights * d_probs, axis=-1, keepdims=True)) * score_scale
    ).astype(jnp.bfloat16)
    masked_scores = member_half[:, :, None, None] * d_scores[None]
    d_queries = jnp.einsum(
        "kthj,kjhd->thd", masked_scores, slot_keys, preferred_element_type=jnp.float32
    )
    d_queries = d_queries.astype(jnp.bfloat16).reshape(tokens, width_local)
    key_slots = jnp.einsum(
        "kthj,thd->kjhd", masked_scores, query_heads, preferred_element_type=jnp.float32
    )
    value_slots = jnp.einsum(
        "kthj,thd->kjhd", masked_probs, d_attended, preferred_element_type=jnp.float32
    )
    slot_terms = jnp.concatenate(
        [
            key_slots.reshape(slot_count, cap_len, width_local),
            value_slots.reshape(slot_count, cap_len, width_local),
        ],
        axis=-1,
    )
    wanted = jnp.arange(caps_local * lax.axis_size("fsdp"), dtype=jnp.int32)
    placing = ((slot_caption[None, :] == wanted[:, None]) & slot_valid[None, :]).astype(jnp.float32)
    kv_grads = lax.psum_scatter(
        jnp.einsum("ck,kjw->cjw", placing, slot_terms).astype(jnp.bfloat16),
        "fsdp",
        scatter_dimension=0,
        tiled=True,
    ).astype(jnp.float32)
    key_grad = kv_grads[:, :, :width_local].astype(jnp.bfloat16)
    value_grad = kv_grads[:, :, width_local:].astype(jnp.bfloat16)
    query_grad = lax.psum_scatter(
        contract_first(video_normed, d_queries).astype(jnp.bfloat16),
        "fsdp",
        scatter_dimension=0,
        tiled=True,
    ).astype(jnp.float32)
    out_weight_grad = lax.psum_scatter(
        contract_first(attended, out_grad).astype(jnp.bfloat16),
        "fsdp",
        scatter_dimension=1,
        tiled=True,
    ).astype(jnp.float32)
    d_normed = contract_last(d_queries, lax.all_gather(cross_query, "fsdp", axis=0, tiled=True))
    d_full = lax.psum(d_normed.astype(jnp.bfloat16), "grp").astype(jnp.float32)
    first_mean = jnp.mean(d_full, axis=-1, keepdims=True)
    second_mean = jnp.mean(d_full * video_hat, axis=-1, keepdims=True)
    full_grad = out_grad.astype(jnp.float32) + inverse * (
        d_full - first_mean - video_hat * second_mean
    )
    input_grad = lax.dynamic_slice_in_dim(full_grad, feature_start, slice_width, 1).astype(
        jnp.bfloat16
    )
    return (updated, input_grad, query_grad, out_weight_grad, key_grad, value_grad)


def solution(mesh):
    in_specs = (
        P("fsdp", None, None),
        P(),
        P(),
        P(None, "grp"),
        P(None, "grp"),
        P(None, "grp"),
        P("grp", None, None),
        P("grp", None),
        P(),
        P("fsdp", "grp"),
        P("fsdp", "grp"),
        P("fsdp", None),
        P(),
        P(),
        P("fsdp", "grp"),
        P("grp", "fsdp"),
        P("fsdp", None),
    )
    out_specs = (
        P("fsdp", "grp"),
        P("fsdp", "grp"),
        P("fsdp", "grp"),
        P("grp", "fsdp"),
        P("fsdp", None, "grp"),
        P("fsdp", None, "grp"),
    )
    return jax.shard_map(local, mesh=mesh, in_specs=in_specs, out_specs=out_specs, check_vma=False)
```

profile of v0, /device:TPU:1, one launch (start us, length us, event | category | flops | bytes accessed | tf_op | source)
XLA Modules:
  0.0 1617.4 jit_solution(3267794305121958579)
XLA Ops:
  8.0 1.2 dynamic_slice.10
  9.3 0.6 iota_compare_fusion.4
  9.9 1.5 fusion.1
  11.5 3.4 convolution_convert_fusion.10
  15.0 2.9 convolution_convert_fusion.9
  18.1 3.0 convolution_convert_fusion.11
  22.0 3.9 convolution_convert_fusion
  27.7 0.7 all-gather.15.cloned.1.call-update
  28.5 54.0 %all-reduce.3.cloned.1.call-done = bf16[128,4096]{1,0:T(8,128)(2,1)} async-done(((bf16[128,4096]{1,0:T(8,128)(2,1)}), bf16[128,4096]{1,0:T(8,128)(2,1)}) %all-reduce.3.cloned.1.call-update) | async-done | bytes 1048592 | tf_op jit(solution)/shard_map/psum | solution.py:78
  82.5 1.6 multiply_reduce_fusion.2
  84.1 93.1 %all-gather.9.cloned.1.call-done = bf16[4096,384]{1,0:T(8,128)(2,1)} async-done(((bf16[128,384]{1,0:T(8,128)(2,1)}), bf16[4096,384]{1,0:T(8,128)(2,1)}) %all-gather.9.cloned.1.call-update) | async-done | bytes 3145744 | tf_op jit(solution)/shard_map/all_gather | solution.py:89
  177.2 3.6 convolution_convert_fusion.13
  181.0 160.0 %all-gather.11.cloned.1.call-done = bf16[4096,384]{1,0:T(8,128)(2,1)} async-done(((bf16[128,384]{1,0:T(8,128)(2,1)}), bf16[4096,384]{1,0:T(8,128)(2,1)}) %all-gather.11.cloned.1.call-update) | async-done | bytes 3145744 | tf_op jit(solution)/shard_map/all_gather | solution.py:84
  341.0 3.6 convolution_convert_fusion.12
  345.7 0.6 iota_add_fusion.1
  348.5 150.5 %all-gather.13.cloned.1.call-done = bf16[3072,384]{1,0:T(8,128)(2,1)} async-done(((bf16[96,384]{1,0:T(8,128)(2,1)}), bf16[3072,384]{1,0:T(8,128)(2,1)}) %all-gather.13.cloned.1.call-update) | async-done | bytes 2359312 | tf_op jit(solution)/shard_map/all_gather | solution.py:131
  499.0 2.7 convolution_convert_fusion.7
  501.7 0.8 copy.110
  502.5 155.5 %all-gather.15.cloned.1.call-done = bf16[384,3072]{0,1:T(8,128)(2,1)} async-done(((bf16[384,96]{0,1:T(8,128)(2,1)}), bf16[384,3072]{0,1:T(8,128)(2,1)}) %all-gather.15.cloned.1.call-update) | async-done | bytes 2359312 | tf_op jit(solution)/shard_map/all_gather | solution.py:151
  658.0 2.6 convolution_convert_fusion.6
  660.7 0.8 copy.115
  661.5 161.5 %all-gather.17.cloned.1.call-done = bf16[4096,384]{1,0:T(8,128)(2,1)} async-done(((bf16[128,384]{1,0:T(8,128)(2,1)}), bf16[4096,384]{1,0:T(8,128)(2,1)}) %all-gather.17.cloned.1.call-update) | async-done | bytes 3145744 | tf_op jit(solution)/shard_map/all_gather | solution.py:96
  823.0 3.2 gather_fusion
  826.2 160.9 %all-gather.19.cloned.1.call-done = bf16[4096,384]{1,0:T(8,128)(2,1)} async-done(((bf16[128,384]{1,0:T(8,128)(2,1)}), bf16[4096,384]{1,0:T(8,128)(2,1)}) %all-gather.19.cloned.1.call-update) | async-done | bytes 3145744 | tf_op jit(solution)/shard_map/all_gather | solution.py:95
  987.1 3.2 gather_fusion.1
  990.3 1.9 broadcast_select_fusion
  992.2 1.8 copy.109
  994.1 0.9 copy.108
  995.0 1.5 fusion.7
  996.4 1.8 fusion.60
  998.2 1.1 copy.113
  999.3 1.4 fusion.8
  1000.7 1.9 fusion.14
  1002.7 1.1 copy.118
  1003.8 1.0 broadcast_multiply_fusion
  1004.8 1.3 fusion.16
  1006.1 0.7 copy-done.7
  1006.7 2.2 convolution_convert_fusion.3
  1009.0 1.5 fusion.15
  1010.5 3.9 convolution_convert_fusion.4
  1014.4 2.5 convolution_convert_fusion.1
  1017.0 0.9 copy-done.8
  1017.9 2.6 convolution_convert_fusion.2
  1020.8 1.2 broadcast_compare_fusion
  1022.3 0.7 copy.120
  1023.1 1.2 copy.122
  1024.3 1.4 convolution_bitcast_fusion
  1025.7 0.7 copy.121
  1026.4 1.9 copy.123
  1028.3 2.9 convolution_convert_fusion.5
  1031.3 6.2 copy.124
  1037.5 2.1 convert_element_type.141
  1039.6 40.5 %all-reduce.5.cloned.1.call-done = bf16[256,3072]{1,0:T(8,128)(2,1)} async-done(((bf16[256,3072]{1,0:T(8,128)(2,1)}), bf16[256,3072]{1,0:T(8,128)(2,1)}) %all-reduce.5.cloned.1.call-update) | async-done | bytes 1572880 | tf_op jit(solution)/shard_map/psum | solution.py:212
  1080.1 1.9 convert_element_type.174
  1082.0 1.1 convert_reduce_fusion.1
  1083.1 1.0 fusion.20
  1084.1 33.1 %reduce-scatter.5.cloned.1.call-done = bf16[256,768]{1,0:T(8,128)(2,1)} async-done(((bf16[256,3072]{1,0:T(8,128)(2,1)}), bf16[256,768]{1,0:T(8,128)(2,1)}) %reduce-scatter.5.cloned.1.call-update) | async-done | bytes 393232 | tf_op jit(solution)/shard_map/reduce_scatter | solution.py:154
  1117.2 2.1 add_convert_fusion
  1119.2 141.6 %reduce-scatter.9.cloned.1.call-done = bf16[384,96]{0,1:T(8,128)(2,1)} async-done(((bf16[384,3072]{0,1:T(8,128)(2,1)}), bf16[384,96]{0,1:T(8,128)(2,1)}) %reduce-scatter.9.cloned.1.call-update) | async-done | bytes 73744 | tf_op jit(solution)/shard_map/reduce_scatter | solution.py:205
  1260.9 1.6 convert_element_type.179
  1262.4 164.3 %reduce-scatter.7.cloned.1.call-done = bf16[96,384]{1,0:T(8,128)(2,1)} async-done(((bf16[3072,384]{1,0:T(8,128)(2,1)}), bf16[96,384]{1,0:T(8,128)(2,1)}) %reduce-scatter.7.cloned.1.call-update) | async-done | bytes 73744 | tf_op jit(solution)/shard_map/reduce_scatter | solution.py:199
  1426.7 1.6 convert_element_type.177
  1428.2 180.1 %reduce-scatter.11.cloned.1.call-done = bf16[1,128,768]{2,1,0:T(8,128)(2,1)} async-done(((bf16[32,128,768]{2,1,0:T(8,128)(2,1)}), bf16[1,128,768]{2,1,0:T(8,128)(2,1)}) %reduce-scatter.11.cloned.1.call-update) | async-done | bytes 196624 | tf_op jit(solution)/shard_map/reduce_scatter | solution.py:191
  1608.3 1.6 fusion.59
  (86 shorter events, 7.1 us)
Async XLA Ops:
  8.0 74.5 %all-reduce.3.cloned.1.call-start = ((), (), s32[]{:S(2)}) async-start(), calls=%async_computation.4 | async-start | bytes 2097152 | tf_op jit(solution)/shard_map/psum | solution.py:78
  11.5 3.5 copy-start.2
  11.5 3.5 copy-start.14
  18.1 3.2 copy-start.6
  25.9 151.3 %copy-start.15 = (f32[4096]{0:T(1024)S(1)}, f32[4096]{0:T(1024)}, u32[]{:S(2)}) copy-start(f32[4096]{0:T(1024)} %param.27) | copy-start | bytes 49156
  25.9 151.3 %all-gather.9.cloned.1.call-start = ((), (), s32[]{:S(2)}) async-start(), calls=%async_computation.5 | async-start | bytes 3244032 | tf_op jit(solution)/shard_map/all_gather | solution.py:89
  26.5 314.5 %all-gather.11.cloned.1.call-start = ((), (), s32[]{:S(2)}) async-start(), calls=%async_computation.6 | async-start | bytes 3244032 | tf_op jit(solution)/shard_map/all_gather | solution.py:84
  27.1 471.9 %all-gather.13.cloned.1.call-start = ((), (), s32[]{:S(2)}) async-start(), calls=%async_computation.7 | async-start | bytes 2433024 | tf_op jit(solution)/shard_map/all_gather | solution.py:131
  27.7 630.4 %all-gather.15.cloned.1.call-start = ((), (), s32[]{:S(2)}) async-start(), calls=%async_computation.8 | async-start | bytes 2433024 | tf_op jit(solution)/shard_map/all_gather | solution.py:151
  28.4 794.6 %all-gather.17.cloned.1.call-start = ((), (), s32[]{:S(2)}) async-start(), calls=%async_computation.14 | async-start | bytes 3244032 | tf_op jit(solution)/shard_map/all_gather | solution.py:96
  180.9 164.0 %copy-start.11 = (s32[32]{0:T(128)S(1)}, s32[32]{0:T(128)}, u32[]{:S(2)}) copy-start(s32[32]{0:T(128)} %param.31) | copy-start | bytes 388
  180.9 165.5 %copy-start.16 = (s32[32]{0:T(128)S(1)}, s32[32]{0:T(128)}, u32[]{:S(2)}) copy-start(s32[32]{0:T(128)} %param.32) | copy-start | bytes 388
  180.9 165.7 %copy-start.17 = (s32[32]{0:T(128)S(1)}, s32[32]{0:T(128)}, u32[]{:S(2)}) copy-start(s32[32]{0:T(128)} %param.20) | copy-start | bytes 388
  180.9 166.0 %copy-start = (bf16[256,3072]{1,0:T(8,128)(2,1)S(1)}, bf16[256,3072]{1,0:T(8,128)(2,1)}, u32[]{:S(2)}) copy-start(bf16[256,3072]{1,0:T(8,128)(2,1)} %param.30) | copy-start | bytes 4718596
  180.9 806.2 %all-gather.19.cloned.1.call-start = ((), (), s32[]{:S(2)}) async-start(), calls=%async_computation.15 | async-start | bytes 3244032 | tf_op jit(solution)/shard_map/all_gather | solution.py:95
  344.6 735.5 %all-reduce.5.cloned.1.call-start = ((), (), s32[]{:S(2)}) async-start(), calls=%async_computation.10 | async-start | bytes 3145728 | tf_op jit(solution)/shard_map/psum | solution.py:212
  346.6 155.1 %copy-start.12 = (s32[3]{0:T(128)}, s32[3]{0:T(128)S(1)}, u32[]{:S(2)}) copy-start(s32[3]{0:T(128)S(1)} %select_reduce_fusion.1) | copy-start | bytes 40
  348.5 309.5 %copy-start.3 = (bf16[256,3072]{1,0:T(8,128)(2,1)S(1)}, bf16[256,3072]{1,0:T(8,128)(2,1)}, u32[]{:S(2)}) copy-start(bf16[256,3072]{1,0:T(8,128)(2,1)} %param.35) | copy-start | bytes 4718596
  995.0 4.4 copy-start.9
  999.3 6.7 copy-start.5
  1003.7 3.0 copy-start.4
  1006.1 0.7 copy-start.7
  1008.9 108.2 %reduce-scatter.5.cloned.1.call-start = ((), (), s32[]{:S(2)}) async-start(), calls=%async_computation.9 | async-start | bytes 1966080 | tf_op jit(solution)/shard_map/reduce_scatter | solution.py:154
  1014.4 246.5 %reduce-scatter.9.cloned.1.call-start = ((), (), s32[]{:S(2)}) async-start(), calls=%async_computation.12 | async-start | bytes 2433024 | tf_op jit(solution)/shard_map/reduce_scatter | solution.py:205
  1017.0 0.9 copy-start.8
  1017.0 409.7 %reduce-scatter.7.cloned.1.call-start = ((), (), s32[]{:S(2)}) async-start(), calls=%async_computation.11 | async-start | bytes 2433024 | tf_op jit(solution)/shard_map/reduce_scatter | solution.py:199
  1020.5 1.5 copy-start.10
  1020.5 7.9 copy-start.13
  1020.5 587.8 %reduce-scatter.11.cloned.1.call-start = ((), (), s32[]{:S(2)}) async-start(), calls=%async_computation.13 | async-start | bytes 6488064 | tf_op jit(solution)/shard_map/reduce_scatter | solution.py:191
  1080.1 1.9 copy-start.1
Sparse Core Ops, SparseCore 0:
  26.1 56.3 all-reduce.2
  1009.1 70.9 all-reduce.4
  1082.9 34.2 reduce-scatter.4
  1119.4 141.4 reduce-scatter.8
  1263.1 163.5 reduce-scatter.6
  1428.9 179.2 reduce-scatter.10
Sparse Core Ops, SparseCore 1:
  28.2 149.0 all-gather.8
  178.9 162.1 all-gather.10
  342.6 156.3 all-gather.12
  500.8 157.2 all-gather.14
  660.4 162.6 all-gather.16
  825.4 161.7 all-gather.18
where the time goes:
time: 1640 us; the launch traced here: 1620 us
  waiting for transfers between devices  1500 us (91%)
  matrix products  47.9 us (3%)
  local copies, waits for them, and re-layouts  29.4 us (2%)
  other arithmetic  25.8 us (2%)
    reduce_scatter x1, waiting for transfers between devices, local(): lax.psum_scatter(jnp.einsum('ck,kjw->cjw', placing, slot_terms).astype(jn...  180 us
    reduce_scatter x1, waiting for transfers between devices, local(): lax.psum_scatter(contract_first(video_normed, d_queries).astype(jnp.bfloa...  164 us
    all_gather x1, waiting for transfers between devices, local(): lax.all_gather(cap_values, 'fsdp', axis=0, tiled=True)  162 us
    all_gather x1, waiting for transfers between devices, local(): lax.all_gather(cap_keys, 'fsdp', axis=0, tiled=True)  161 us
    all_gather x1, waiting for transfers between devices, local(): lax.all_gather(cross_key, 'fsdp', axis=0, tiled=True)  160 us
    all_gather x1, waiting for transfers between devices, local(): lax.all_gather(cross_out, 'fsdp', axis=1, tiled=True)  156 us
    all_gather x1, waiting for transfers between devices, local(): lax.all_gather(cross_query, 'fsdp', axis=0, tiled=True)  150 us
    reduce_scatter x1, waiting for transfers between devices, local(): lax.psum_scatter(contract_first(attended, out_grad).astype(jnp.bfloat16),...  142 us
  transfers between devices with their start and end apart: 12, of which 12 were waited for; matrix products, arithmetic and copies ran while one was open for 4% of the time, Pallas kernels for 0%

commit v1 on v0

v1 whole, which is shorter than its diff:
```python
import functools, math
import jax, jax.numpy as jnp
from jax import lax
from jax.experimental import pallas as pl
from jax.experimental.pallas import tpu as pltpu
from jax.sharding import PartitionSpec as P
MESH = pl.DeviceIdType.MESH

class Links:
    def __init__(self, sems):
        self.sems, self.keys, self.pending = sems, {}, []
    def sem(self, key):
        return self.sems.at[self.keys.setdefault(key, len(self.keys))]
    def copy(self, src, dst, key, dev):
        c = pltpu.make_async_remote_copy(src_ref=src, dst_ref=dst, send_sem=self.sem(("s", key)), recv_sem=self.sem(("r", key)), device_id=dev, device_id_type=MESH)
        return c
    def send(self, src, dst, key, dev):
        c = self.copy(src, dst, key, dev)
        c.start()
        self.pending.append(c)
    def recv(self, dst, key, dev):
        self.copy(dst, dst, key, dev).wait_recv()
    def drain(self):
        for c in self.pending:
            c.wait_send()
        self.pending = []

def place():
    g, f = lax.axis_index("grp"), lax.axis_index("fsdp")
    return dict(hi=g // 2, core=g % 2, y=f // 8, z=(f // 2) % 4, x=f % 2, g=g, f=f)

def dev(hi, core, y, z, x):
    return {"grp": hi * 2 + core, "fsdp": (y * 4 + z) * 2 + x}

class Gather:
    def __init__(self, L, me, name, G, rows):
        self.L, self.me, self.name, self.G, self.rows = L, me, name, G, rows
    def nb(self, part, first, d):
        m = self.me
        use_z = (m["x"] == 0) if (part == 0) == first else (m["x"] == 1)
        zi = jnp.where(use_z, (m["z"] + d) % 4, m["z"])
        yi = jnp.where(use_z, m["y"], (m["y"] + d) % 4)
        return {"fsdp": (yi * 4 + zi) * 2 + m["x"], "grp": m["g"]}
    def idx(self, part, d1, d2):
        m = self.me
        use_z = (m["x"] == 0) if part == 0 else (m["x"] == 1)
        dz = jnp.where(use_z, d1, d2)
        dy = jnp.where(use_z, d2, d1)
        px = m["x"] if part == 0 else 1 - m["x"]
        return (((m["y"] + dy) % 4) * 4 + (m["z"] + dz) % 4) * 2 + px
    def ref(self, part, d1, d2, half=None):
        b = self.G.at[self.idx(part, d1, d2)]
        if half is None:
            return b
        h = self.rows // 2
        return b.at[pl.ds(half * h, h)]
    def xsend(self, src):
        m = self.me
        self.L.send(src, self.G.at[m["f"]], (self.name, "x"), {"grp": m["g"], "fsdp": m["f"] + 1 - 2 * m["x"]})
    def xrecv(self):
        m = self.me
        self.L.recv(self.ref(1, 0, 0), (self.name, "x"), {"grp": m["g"], "fsdp": m["f"] + 1 - 2 * m["x"]})
    def s1(self, part, first, k, src=None):
        d = (0, 0) if first else (k, 0)
        r = self.ref(part, *d)
        src = r if src is None else src
        for s in (1, 3):
            self.L.send(src, r, (self.name, part, first, k, "s1", s), self.nb(part, first, s))
    def s2(self, part, first, k, s):
        o = 4 - s
        d = (o, 0) if first else (k, o)
        self.L.recv(self.ref(part, *d), (self.name, part, first, k, "s1", s), self.nb(part, first, o))
        half = 0 if s == 1 else 1
        r = self.ref(part, *d, half)
        self.L.send(r, r, (self.name, part, first, k, "s2", s), self.nb(part, first, s))
    def s3(self, part, first, k):
        d = (2, 0) if first else (k, 2)
        for s in (1, 3):
            half = 0 if s == 1 else 1
            self.L.recv(self.ref(part, *d, half), (self.name, part, first, k, "s2", s), self.nb(part, first, 4 - s))
    def run(self, own, xsrc):
        for st in self.stages(own, xsrc):
            st()
    def stages(self, own, xsrc):
        def a():
            self.xsend(xsrc); self.s1(0, True, 0, own)
        def b():
            self.xrecv(); self.s1(1, True, 0)
        def c():
            self.s2(0, True, 0, 1); self.s2(0, True, 0, 3)
            self.s1(0, False, 0, own)
            self.s2(1, True, 0, 1); self.s2(1, True, 0, 3)
            self.s1(1, False, 0)
        def d():
            for k in (1, 3):
                self.s1(0, False, k); self.s1(1, False, k)
        def e():
            self.s3(0, True, 0); self.s1(0, False, 2)
            self.s3(1, True, 0); self.s1(1, False, 2)
        def fw(k):
            def f():
                for part in (0, 1):
                    self.s2(part, False, k, 1); self.s2(part, False, k, 3)
            return f
        def fin(k):
            def f():
                for part in (0, 1):
                    self.s3(part, False, k)
            return f
        return [a, b, c, d, e, fw(0), fw(1), fin(0), fw(3), fin(1), fw(2), fin(3), fin(2)]

def barrier(me, devs):
    b = pltpu.get_barrier_semaphore()
    for d in devs:
        pl.semaphore_signal(b, inc=1, device_id=d, device_id_type=MESH)
    pl.semaphore_wait(b, len(devs))

def neighbours(me):
    m = me
    out = [{"grp": m["g"], "fsdp": m["f"] + 1 - 2 * m["x"]}]
    for d in (1, 3):
        out.append({"grp": m["g"], "fsdp": (m["y"] * 4 + (m["z"] + d) % 4) * 2 + m["x"]})
        out.append({"grp": m["g"], "fsdp": (((m["y"] + d) % 4) * 4 + m["z"]) * 2 + m["x"]})
    return out


class TwoStep:
    def __init__(self, L, me, name, parts, r1, s1, r2):
        self.L, self.me, self.name = L, me, name
        self.parts, self.r1, self.s1, self.r2 = parts, r1, s1, r2
        self.sib = {"grp": me["g"] + 1 - 2 * me["core"], "fsdp": me["f"]}
        self.opp = {"grp": (1 - me["hi"]) * 2 + me["core"], "fsdp": me["f"]}
    def start(self):
        other = 1 - self.me["core"]
        for j in range(2):
            h = 1 - self.me["hi"] if j == 0 else self.me["hi"]
            self.L.send(self.parts.at[2 * h + other], self.r1.at[j], (self.name, "c", j), self.sib)
    def mid(self):
        m = self.me
        self.L.recv(self.r1.at[0], (self.name, "c", 0), self.sib)
        self.s1[...] = (self.parts[2 * (1 - m["hi"]) + m["core"]].astype(jnp.float32) + self.r1[0].astype(jnp.float32)).astype(jnp.bfloat16)
        self.L.send(self.s1, self.r2, (self.name, "o"), self.opp)
    def end(self):
        m = self.me
        self.L.recv(self.r1.at[1], (self.name, "c", 1), self.sib)
        self.L.recv(self.r2, (self.name, "o"), self.opp)
        return self.parts[2 * m["hi"] + m["core"]].astype(jnp.float32) + self.r1[1].astype(jnp.float32) + self.r2[...].astype(jnp.float32)


def along_x(me, d):
    X = (me["hi"] * 2 + me["x"] + d) % 4
    return X // 2, X % 2


def same_core(me, d):
    hi, x = along_x(me, d)
    return dev(hi, me["core"], me["y"], me["z"], x)


class Eight:
    def __init__(self, L, me, name, E, rows):
        self.L, self.me, self.name, self.E, self.rows = L, me, name, E, rows
        self.sib = {"grp": me["g"] + 1 - 2 * me["core"], "fsdp": me["f"]}
    def ref(self, d, core, half=None):
        hi, x = along_x(self.me, d)
        r = self.E.at[x, hi * 2 + core]
        if half is None:
            return r
        h = self.rows // 2
        return r.at[pl.ds(half * h, h)]
    def start(self):
        r = self.ref(0, self.me["core"])
        for s in (1, 3):
            self.L.send(r, r, (self.name, "s1", s), same_core(self.me, s))
        self.L.send(r, r, (self.name, "sib", 0), self.sib)
    def mid(self):
        c = self.me["core"]
        for s in (1, 3):
            r = self.ref(4 - s, c)
            self.L.recv(r, (self.name, "s1", s), same_core(self.me, s))
            half = 0 if s == 1 else 1
            rh = self.ref(4 - s, c, half)
            self.L.send(rh, rh, (self.name, "s2", s), same_core(self.me, s))
            self.L.send(r, r, (self.name, "sib", 4 - s), self.sib)
    def mid2(self):
        c = self.me["core"]
        for s in (1, 3):
            half = 0 if s == 1 else 1
            rh = self.ref(2, c, half)
            self.L.recv(rh, (self.name, "s2", s), same_core(self.me, s))
            self.L.send(rh, rh, (self.name, "sib2", s), self.sib)
    def end(self):
        oc = 1 - self.me["core"]
        for d in (0, 1, 3):
            self.L.recv(self.ref(d, oc), (self.name, "sib", d), self.sib)
        for s in (1, 3):
            self.L.recv(self.ref(2, oc, 0 if s == 1 else 1), (self.name, "sib2", s), self.sib)


def eight_others(me):
    out = []
    for d in range(4):
        hi, x = along_x(me, d)
        for c in (0, 1):
            if d == 0 and c == 0:
                continue
            core = 1 - me["core"] if c == 1 else me["core"]
            out.append(((d, c), dev(hi, core, me["y"], me["z"], x), (x, hi * 2 + core)))
    return out


class Scatter:
    def __init__(self, L, me, name, D, ra, rb, rx):
        self.L, self.me, self.name, self.D, self.ra, self.rb, self.rx = L, me, name, D, ra, rb, rx
        self.rows = D.shape[1]
    def axis(self, part, stage):
        m = self.me
        own = m["x"] == 0 if part == 0 else m["x"] == 1
        return own if stage == 1 else jnp.logical_not(own)
    def nb(self, part, stage, d):
        m = self.me
        use_z = self.axis(part, stage)
        zi = jnp.where(use_z, (m["z"] + d) % 4, m["z"])
        yi = jnp.where(use_z, m["y"], (m["y"] + d) % 4)
        return {"fsdp": (yi * 4 + zi) * 2 + m["x"], "grp": m["g"]}
    def ref(self, part, stage, k, d, half=None):
        m = self.me
        use_z = self.axis(part, stage)
        dz = jnp.where(use_z, d, k)
        dy = jnp.where(use_z, k, d)
        px = m["x"] if part == 0 else 1 - m["x"]
        b = self.D.at[(((m["y"] + dy) % 4) * 4 + (m["z"] + dz) % 4) * 2 + px]
        if half is None:
            return b
        h = self.rows // 2
        return b.at[pl.ds(half * h, h)]
    def slot(self, stage, k):
        return k if stage == 0 else 4
    def far(self, part, stage, k):
        h = self.rows // 2
        for s in (1, 3):
            half = 0 if s == 1 else 1
            self.L.send(self.ref(part, stage, k, 2, half), self.ra.at[part, self.slot(stage, k), pl.ds(half * h, h)], (self.name, part, stage, k, "far", s), self.nb(part, stage, s))
    def near(self, part, stage, k):
        h = self.rows // 2
        for s in (1, 3):
            half = 0 if s == 1 else 1
            buf = self.ra.at[part, self.slot(stage, k), pl.ds(half * h, h)]
            self.L.recv(buf, (self.name, part, stage, k, "far", s), self.nb(part, stage, 4 - s))
            r = self.ref(part, stage, k, s, half)
            r[...] = (r[...].astype(jnp.float32) + buf[...].astype(jnp.float32)).astype(jnp.bfloat16)
            self.L.send(self.ref(part, stage, k, s), self.rb.at[part, self.slot(stage, k), half], (self.name, part, stage, k, "near", s), self.nb(part, stage, s))
    def total(self, part, stage, k):
        for s in (1, 3):
            half = 0 if s == 1 else 1
            self.L.recv(self.rb.at[part, self.slot(stage, k), half], (self.name, part, stage, k, "near", s), self.nb(part, stage, 4 - s))
        b = self.rb.at[part, self.slot(stage, k)]
        return self.ref(part, stage, k, 0)[...].astype(jnp.float32) + b[0].astype(jnp.float32) + b[1].astype(jnp.float32)
    def fold(self, part, stage, k):
        t = self.total(part, stage, k)
        self.ref(part, stage, k, 0)[...] = t.astype(jnp.bfloat16)
    def partner(self):
        m = self.me
        return {"grp": m["g"], "fsdp": m["f"] + 1 - 2 * m["x"]}
    def xsend(self):
        self.fold(1, 1, 0)
        self.L.send(self.ref(1, 1, 0, 0), self.rx, (self.name, "x"), self.partner())
    def result(self):
        t = self.total(0, 1, 0)
        self.L.recv(self.rx, (self.name, "x"), self.partner())
        return t + self.rx[...].astype(jnp.float32)
    def stages(self):
        def a():
            for k in (2, 1, 3, 0):
                for part in (1, 0):
                    self.far(part, 0, k)
        def b(k):
            def f():
                for part in (1, 0):
                    self.near(part, 0, k)
            return f
        def c(k):
            def f():
                for part in (1, 0):
                    self.fold(part, 0, k)
                    if k == 2:
                        self.far(part, 1, 0)
            return f
        def d():
            for part in (1, 0):
                self.near(part, 1, 0)
        return [a, b(2), b(1), c(2), b(3), c(1), b(0), c(3), d, c(0), self.xsend]


class Spread:
    def __init__(self, L, me, name, src, dst, send_sem, recv_sem):
        self.me, self.src, self.dst, self.ss, self.rs = me, src, dst, send_sem, recv_sem
    def copy(self, j):
        m = self.me
        to = (m["f"] + j) % 32
        return pltpu.make_async_remote_copy(src_ref=self.src(to), dst_ref=self.dst(m["f"]), send_sem=self.ss, recv_sem=self.rs, device_id={"grp": m["g"], "fsdp": to}, device_id_type=MESH)
    def start(self):
        @pl.loop(1, 32)
        def _(j):
            self.copy(j).start()


def wait_bytes(like, send_sem, recv_sem, devid, recv=True, send=True):
    c = pltpu.make_async_remote_copy(src_ref=like, dst_ref=like, send_sem=send_sem, recv_sem=recv_sem, device_id=devid, device_id_type=MESH)
    if recv:
        c.wait_recv()
    if send:
        c.wait_send()


def V():
    return pl.BlockSpec(memory_space=pltpu.VMEM)


def S():
    return pl.BlockSpec(memory_space=pltpu.SMEM)


def call(kernel, name, cid, n_in, outs, scratch, smem=()):
    return pl.pallas_call(
        kernel,
        out_shape=tuple(jax.ShapeDtypeStruct(s, d) for s, d in outs),
        in_specs=[S() if i in smem else V() for i in range(n_in)],
        out_specs=tuple(V() for _ in outs),
        scratch_shapes=scratch,
        compiler_params=pltpu.CompilerParams(collective_id=cid, has_side_effects=True, vmem_limit_bytes=60 << 20),
        name=name,
    )


BF, F32 = jnp.bfloat16, jnp.float32
DMA = pltpu.SemaphoreType.DMA


def k1(kv, qo, parts, cs, fgain, gw, gq, E, SS, r1, s1, r2, sems):
    me = place()
    L = Links(sems)
    others = eight_others(me)
    barrier(me, [d for _, d, _ in others] + neighbours(me)[1:])
    A, B = Gather(L, me, "w", gw, 128), Gather(L, me, "q", gq, 192)
    sa, sb = A.stages(kv.at[me["x"]], kv.at[1 - me["x"]]), B.stages(qo, qo)
    T = TwoStep(L, me, "t", parts, r1, s1, r2)
    X = Eight(L, me, "e", E, 128)
    T.start()
    sa[0]()
    gw[me["f"]] = kv[me["x"]]
    gq[me["f"]] = qo[...]
    sa[1]()
    T.mid()
    sa[2]()
    sa[3]()
    total = T.end()
    ts = total + cs[...].astype(F32)
    E[me["x"], me["g"]] = (ts * fgain[...]).astype(BF)
    ss = jnp.sum(ts * ts, axis=1, keepdims=True)
    SS[me["x"], me["g"]] = jnp.broadcast_to(ss, (128, 128)).T[:8]
    X.start()
    r = SS.at[me["x"], me["g"]]
    for key, d, _ in others:
        L.send(r, r, ("ss", (4 - key[0]) % 4, key[1]), d)
    sa[4]()
    X.mid()
    sa[5]()
    X.mid2()
    rest = []
    for i in range(8):
        if 6 + i < len(sa):
            sa[6 + i]()
        sb[i]()
    X.end()
    for key, d, slot in others:
        L.recv(SS.at[slot[0], slot[1]], ("ss", key[0], key[1]), d)
    for b in sb[8:]:
        b()
    L.drain()


def k2(kvp, cap, R, C, sb, s1, r1, s2, r2):
    me = place()
    partner = {"grp": me["g"], "fsdp": (me["f"] + 1) % 32}
    barrier(me, [{"grp": me["g"], "fsdp": (me["f"] + j) % 32} for j in range(1, 32)])
    yz = me["f"] // 2

    def p1(j):
        to = (yz + j) % 16
        return pltpu.make_async_remote_copy(src_ref=kvp.at[to], dst_ref=C.at[pl.ds(2 * yz, 2)], send_sem=s1, recv_sem=r1, device_id={"grp": me["g"], "fsdp": to * 2 + me["x"]}, device_id_type=MESH)

    @pl.loop(1, 16)
    def _(j):
        p1(j).start()
    C[pl.ds(2 * yz, 2)] = kvp[yz]
    wait_bytes(C.at[pl.ds(0, 30)], s1, r1, partner)

    def p2(j):
        to = (me["f"] + j) % 32
        return to, pltpu.make_async_remote_copy(src_ref=sb.at[to], dst_ref=R.at[me["f"]], send_sem=s2, recv_sem=r2, device_id={"grp": me["g"], "fsdp": to}, device_id_type=MESH)

    @pl.loop(1, 32)
    def _(j):
        to, c = p2(j)
        for s in range(3):
            sb[to, s] = C[cap[to * 3 + s]]
        c.start()
    for s in range(3):
        R[me["f"], s] = C[cap[me["f"] * 3 + s]]
    wait_bytes(R.at[pl.ds(0, 31)], s2, r2, partner)


def k3(d_in, op, dn, vhat, T, idx, G, out_sum, d_sum, stat, KV, D, ra, rb, rx, o1, o2, o3, n1, n2, n3, R, C, s1, r1, s2, r2, sems):
    me = place()
    L = Links(sems)
    partner = {"grp": me["g"], "fsdp": (me["f"] + 1) % 32}
    grp = [{"grp": (me["g"] + j) % 4, "fsdp": me["f"]} for j in range(1, 4)]
    barrier(me, [{"grp": me["g"], "fsdp": (me["f"] + j) % 32} for j in range(1, 32)] + grp)
    D[...] = d_in[...]
    sc = Scatter(L, me, "d", D, ra, rb, rx)
    stages = sc.stages()
    Tn = TwoStep(L, me, "n", dn, n1, n2, n3)
    To = TwoStep(L, me, "o", op, o1, o2, o3)

    @pl.loop(1, 32)
    def _(j):
        to = (me["f"] + j) % 32
        pltpu.make_async_remote_copy(src_ref=T.at[to], dst_ref=R.at[pl.ds(3 * me["f"], 3)], send_sem=s1, recv_sem=r1, device_id={"grp": me["g"], "fsdp": to}, device_id_type=MESH).start()
    stages[0]()
    Tn.start()
    To.start()
    R[pl.ds(96, 3)] = jnp.zeros((3, 8, 384), BF)
    R[pl.ds(3 * me["f"], 3)] = T[me["f"]]
    Tn.mid()
    To.mid()
    stages[1]()
    stages[2]()
    wait_bytes(R.at[pl.ds(0, 93)], s1, r1, partner)

    @pl.loop(0, 32)
    def _(c):
        acc = R[idx[c * 5]].astype(F32)
        for m in range(1, 5):
            acc = acc + R[idx[c * 5 + m]].astype(F32)
        C[c] = acc.astype(BF)

    @pl.loop(1, 32)
    def _(j):
        to = (me["f"] + j) % 32
        pltpu.make_async_remote_copy(src_ref=C.at[to], dst_ref=KV.at[me["f"]], send_sem=s2, recv_sem=r2, device_id={"grp": me["g"], "fsdp": to}, device_id_type=MESH).start()
    KV[me["f"]] = C[me["f"]]
    for s in stages[3:5]:
        s()
    t = Tn.end()
    d_sum[...] = t
    a = jnp.sum(t, axis=1, keepdims=True)
    b = jnp.sum(t * vhat[...], axis=1, keepdims=True)
    stat[me["g"], 0] = jnp.broadcast_to(a, (256, 128)).T[:8]
    stat[me["g"], 1] = jnp.broadcast_to(b, (256, 128)).T[:8]
    mine = stat.at[me["g"]]
    for j in range(1, 4):
        L.send(mine, mine, ("st", j), grp[j - 1])
    for s in stages[5:]:
        s()
    out_sum[...] = To.end()
    G[...] = sc.result()
    for j in range(1, 4):
        L.recv(stat.at[(me["g"] + 4 - j) % 4], ("st", j), grp[3 - j])
    wait_bytes(KV.at[pl.ds(0, 31)], s2, r2, partner)
    L.drain()


HEAD_SIZE = 128


def rms_scale(values, gain):
    mean_square = jnp.mean(values * values, axis=-1, keepdims=True)
    return values * lax.rsqrt(mean_square + 1e-06) * gain


def dot(a, b, ca, cb):
    return lax.dot_general(a, b, (((ca,), (cb,)), ((), ())), preferred_element_type=F32)


def tables(video_counts, sample_caption):
    numbers = jnp.arange(32, dtype=jnp.int32)
    end = jnp.sum(jnp.where(numbers[None, :] <= numbers[:, None], video_counts[None, :], 0), axis=1)
    first = jnp.sum((end[None, :] <= (256 * numbers)[:, None]).astype(jnp.int32), axis=1)
    slot = first[:, None] + jnp.arange(3, dtype=jnp.int32)
    clipped = jnp.minimum(slot, 31)
    cap = jnp.sum(jnp.where(clipped[:, :, None] == numbers, sample_caption, 0), axis=2)
    hit = sample_caption[None, :] == numbers[:, None]
    sample = jnp.sum(jnp.where(hit, numbers[None, :], 0), axis=1)
    stop = jnp.sum(jnp.where(hit, end[None, :], 0), axis=1)
    start = stop - jnp.sum(jnp.where(hit, video_counts[None, :], 0), axis=1)
    d = (start // 256)[:, None] + jnp.arange(5, dtype=jnp.int32)
    first_d = jnp.sum(jnp.where(jnp.minimum(d, 31)[:, :, None] == numbers, first, 0), axis=2)
    idx = jnp.where((d < 32) & (d * 256 < stop[:, None]), 3 * d + sample[:, None] - first_d, 96)
    return end, first, slot, cap, idx.reshape(160)


def local(caption_states, caption_lens, text_gain, text_query, text_key, text_value, text_bias, text_out, final_gain, cross_key, cross_value, video_states, video_counts, sample_caption, cross_query, cross_out, out_grad):
    f, g = lax.axis_index("fsdp"), lax.axis_index("grp")
    flat = caption_states.reshape(128, 4096).astype(F32)
    normed = rms_scale(flat, text_gain).astype(BF)
    heads = lambda w: jnp.dot(normed, w, preferred_element_type=F32).astype(BF).reshape(128, 8, 64)
    tq, tk, tv = heads(text_query), heads(text_key), heads(text_value)
    ts = jnp.einsum("ihd,jhd->hij", tq, tk, preferred_element_type=F32) + text_bias
    mylen = lax.dynamic_slice_in_dim(caption_lens, f, 1)[0]
    e = jnp.where(jnp.arange(128)[None, None, :] < mylen, jnp.exp(ts), 0.0)
    tw = (e / jnp.sum(e, axis=-1, keepdims=True)).astype(BF)
    tm = jnp.einsum("hij,jhd->ihd", tw, tv, preferred_element_type=F32).astype(BF).reshape(128, 512)
    parts = jnp.dot(tm, text_out, preferred_element_type=F32).astype(BF).reshape(128, 4, 1024).transpose(1, 0, 2)
    cs = lax.dynamic_slice_in_dim(caption_states[0], g * 1024, 1024, 1)
    fg = lax.dynamic_slice_in_dim(final_gain, g * 1024, 1024, 0)[None]
    kv = jnp.stack([cross_key, cross_value])
    qo = jnp.concatenate([cross_query, cross_out.T])
    gw, gq, E, SS = call(
        k1, "gather_text", 0, 5,
        [((32, 128, 384), BF), ((32, 192, 384), BF), ((2, 4, 128, 1024), BF), ((2, 4, 8, 128), F32)],
        [pltpu.VMEM((2, 128, 1024), BF), pltpu.VMEM((128, 1024), BF), pltpu.VMEM((128, 1024), BF), DMA((256,))],
    )(kv, qo, parts, cs, fg)
    rstd = lax.rsqrt(jnp.sum(SS[:, :, 0, :], axis=1) / 4096 + 1e-6).reshape(256, 1)
    X = E.transpose(0, 2, 1, 3).reshape(256, 4096)
    kvp = (jnp.dot(X, gw.reshape(4096, 384), preferred_element_type=F32) * rstd).astype(BF)
    kvp = kvp.reshape(2, 16, 8, 384).transpose(1, 0, 2, 3)
    end, first, slot, cap, idx = tables(video_counts, sample_caption)
    (R,) = call(
        k2, "spread_kv", 1, 2, [((32, 3, 8, 384), BF)],
        [pltpu.VMEM((32, 8, 384), BF), pltpu.VMEM((32, 3, 8, 384), BF), DMA, DMA, DMA, DMA],
        smem=(1,),
    )(kvp, cap.reshape(96))
    R = R.reshape(16, 2, 3, 8, 384).transpose(1, 2, 0, 3, 4).reshape(2, 3, 128, 384)
    ks, vs = R[0].reshape(3, 128, 3, 128), R[1].reshape(3, 128, 3, 128)
    positions = f * 256 + jnp.arange(256, dtype=jnp.int32)
    token_sample = jnp.sum((end[None, :] <= positions[:, None]).astype(jnp.int32), axis=1)
    my_slot = lax.dynamic_slice_in_dim(slot, f, 1)[0]
    my_cap = lax.dynamic_slice_in_dim(cap, f, 1)[0]
    lens = jnp.sum(jnp.where(my_cap[:, None] == jnp.arange(32), caption_lens[None, :], 0), axis=1)
    member = token_sample[None, :] == my_slot[:, None]
    token_lens = jnp.sum(jnp.where(member, lens[:, None], 0), axis=0)
    mh = member.astype(BF)
    video = video_states.astype(F32)
    center = video - jnp.mean(video, axis=-1, keepdims=True)
    inverse = lax.rsqrt(jnp.mean(center * center, axis=-1, keepdims=True) + 1e-06)
    vhat = center * inverse
    vn = vhat.astype(BF)
    Wq, WoT = gq[:, :96].reshape(3072, 384), gq[:, 96:].reshape(3072, 384)
    scale = 1.0 / math.sqrt(HEAD_SIZE)
    q = jnp.dot(vn, Wq, preferred_element_type=F32).astype(BF).reshape(256, 3, 128)
    pick = lambda a: jnp.where(member[0][:, None, None], a[0], jnp.where(member[1][:, None, None], a[1], a[2]))
    sc = pick(jnp.einsum("thd,kjhd->kthj", q, ks, preferred_element_type=F32)) * scale
    valid = (jnp.arange(128)[None, :] < token_lens[:, None])[:, None, :]
    ex = jnp.where(valid, jnp.exp(sc), 0.0)
    w = ex / jnp.sum(ex, axis=-1, keepdims=True)
    p = w.astype(BF)
    mp = mh[:, :, None, None] * p[None]
    att = jnp.einsum("kthj,kjhd->thd", mp, vs, preferred_element_type=F32).astype(BF).reshape(256, 384)
    op = dot(att, WoT, 1, 1).astype(BF).reshape(256, 4, 768).transpose(1, 0, 2)
    da = dot(out_grad, WoT, 1, 0).astype(BF).reshape(256, 3, 128)
    dp = pick(jnp.einsum("thd,kjhd->kthj", da, vs, preferred_element_type=F32))
    ds = (w * (dp - jnp.sum(w * dp, axis=-1, keepdims=True)) * scale).astype(BF)
    ms = mh[:, :, None, None] * ds[None]
    dq = jnp.einsum("kthj,kjhd->thd", ms, ks, preferred_element_type=F32).astype(BF).reshape(256, 384)
    kt = jnp.einsum("kthj,thd->kjhd", ms, q, preferred_element_type=F32).astype(BF).reshape(3, 16, 8, 384)
    vt = jnp.einsum("kthj,thd->kjhd", mp, da, preferred_element_type=F32).astype(BF).reshape(3, 16, 8, 384)
    T = jnp.stack([kt, vt]).transpose(2, 0, 1, 3, 4).reshape(32, 3, 8, 384)
    D = jnp.concatenate([dot(vn, dq, 0, 0).astype(BF).reshape(32, 96, 384), dot(out_grad, att, 0, 0).astype(BF).reshape(32, 96, 384)], axis=1)
    dn = dot(dq, Wq, 1, 1).astype(BF).reshape(256, 4, 768).transpose(1, 0, 2)
    cut = lambda a: lax.dynamic_slice_in_dim(a, g * 768, 768, 1)
    vh = cut(vhat)
    half = [pltpu.VMEM((2, 256, 768), BF), pltpu.VMEM((256, 768), BF), pltpu.VMEM((256, 768), BF)]
    G, out_sum, d_sum, stat, KV = call(
        k3, "reduce_grads", 2, 6,
        [((192, 384), F32), ((256, 768), F32), ((256, 768), F32), ((4, 2, 8, 256), F32), ((32, 8, 384), BF)],
        [pltpu.VMEM((32, 192, 384), BF), pltpu.VMEM((2, 5, 192, 384), BF), pltpu.VMEM((2, 5, 2, 192, 384), BF), pltpu.VMEM((192, 384), BF)]
        + half + half + [pltpu.VMEM((99, 8, 384), BF), pltpu.VMEM((32, 8, 384), BF), DMA, DMA, DMA, DMA, DMA((256,))],
        smem=(5,),
    )(D, op, dn, vh, T, idx)
    updated = (cut(video_states).astype(F32) + out_sum).astype(BF)
    mean = jnp.sum(stat[:, :, 0], axis=0) / 3072
    ig = (cut(out_grad).astype(F32) + inverse * (d_sum - mean[0][:, None] - vh * mean[1][:, None])).astype(BF)
    KV = KV.reshape(16, 2, 8, 384)
    return updated, ig, G[:96], G[96:].T, KV[:, 0].reshape(1, 128, 384), KV[:, 1].reshape(1, 128, 384)


def solution(mesh):
    in_specs = (P("fsdp"), P(), P(), P(None, "grp"), P(None, "grp"), P(None, "grp"), P("grp"), P("grp"), P(), P("fsdp", "grp"), P("fsdp", "grp"), P("fsdp"), P(), P(), P("fsdp", "grp"), P("grp", "fsdp"), P("fsdp"))
    out_specs = (P("fsdp", "grp"), P("fsdp", "grp"), P("fsdp", "grp"), P("grp", "fsdp"), P("fsdp", None, "grp"), P("fsdp", None, "grp"))
    return jax.shard_map(local, mesh=mesh, in_specs=in_specs, out_specs=out_specs, check_vma=False)
```

time: 1640 us -> 242 us (0.15); the launches traced: 1620 us -> 238 us
  waiting for transfers between devices: 1500 us -> 0 us
  Pallas kernels: 0 us -> 140 us
    all_gather x6 -> x0, waiting for transfers between devices: 881 us -> none  [the longest x1 162 us: local(): lax.all_gather(cap_values, 'fsdp', axis=0, tiled=True)]
    reduce_scatter x4 -> x0, waiting for transfers between devices: 519 us -> none  [the longest x1 180 us: local(): lax.psum_scatter(jnp.einsum('ck,kjw->cjw', placing, slot_terms).astype(jn...]
    pallas_call x0 -> x3, Pallas kernels: none -> 140 us  [the longest x1 66.4 us: local(): call(k1, 'gather_text', 0, 5, [((32, 128, 384), BF), ((32, 192, 384), BF)...]
    psum x2 -> x0, waiting for transfers between devices: 94.5 us -> none  [the longest x1 54 us: local(): lax.psum(partial_value.astype(jnp.bfloat16), 'grp').astype(jnp.float32)]
    dot_general x21 -> x19, matrix products: 47.9 us -> 33.9 us  [the longest x5 13.8 us: dot(): lax.dot_general(a, b, (((ca,), (cb,)), ((), ())), preferred_element_type=...]
  transfers between devices with their start and end apart: 12 -> 0, of which waited for: 12 -> 0; matrix products, arithmetic and copies ran while one was open for 4% -> 0% of each run, Pallas kernels for 0% -> 0%
where the time goes in v1:
time: 242 us; the launch traced here: 238 us
  Pallas kernels  140 us (58%)
  local copies, waits for them, and re-layouts  43.9 us (18%)
  matrix products  33.9 us (14%)
  other arithmetic  19.3 us (8%)
    pallas_call x1, Pallas kernels, local(): call(k1, 'gather_text', 0, 5, [((32, 128, 384), BF), ((32, 192, 384), BF)...  66.4 us
    pallas_call x1, Pallas kernels, local(): call(k3, 'reduce_grads', 2, 6, [((192, 384), F32), ((256, 768), F32), ((2...  53.5 us
    pallas_call x1, Pallas kernels, local(): call(k2, 'spread_kv', 1, 2, [((32, 3, 8, 384), BF)], [pltpu.VMEM((32, 8,...  20.1 us
    dot_general x5, matrix products, dot(): lax.dot_general(a, b, (((ca,), (cb,)), ((), ())), preferred_element_type=...  13.8 us
    dot_general x3, matrix products, local(): jnp.dot(normed, w, preferred_element_type=F32).astype(BF)  9.32 us
    unnamed x84, local copies, waits for them, and re-layouts  7.59 us
    concatenate x1, other arithmetic, local(): jnp.concatenate([dot(vn, dq, 0, 0).astype(BF).reshape(32, 96, 384), dot(o...  5.22 us

profile of v1, /device:TPU:1, one launch (start us, length us, event | category | flops | bytes accessed | tf_op | source)
XLA Modules:
  0.0 238.4 jit_solution(18137250499724207664)
XLA Ops:
  0.6 1.2 dynamic_slice.27
  1.9 0.6 iota_compare_fusion.6
  2.5 1.5 fusion.4
  4.1 3.4 %convolution_convert_fusion.11 = bf16[128,512]{1,0:T(8,128)(2,1)S(1)} fusion(bf16[4096,512]{1,0:T(8,128)(2,1)} %param.20, bf16[1,128,4096]{2,1,0:T(8,128)(2,1)} %param.17, f32[4096]{0:T(1024)} %param.19, f32[128]{0:T(128)S(1)} %add_rsqrt_fusion.1), kind=kOutput, calls=%fused_computation.36 | convolution fusion | flops 539033600 | bytes 5390848 | tf_op jit(solution)/shard_map/dot_general | solution.py:507
  7.6 3.0 %convolution_convert_fusion.10 = bf16[128,512]{1,0:T(8,128)(2,1)S(1)} fusion(bf16[4096,512]{1,0:T(8,128)(2,1)} %param.21, bf16[1,128,4096]{2,1,0:T(8,128)(2,1)S(1)} %copy-done.5, f32[4096]{0:T(1024)S(1)} %copy-done.39, f32[128]{0:T(128)S(1)} %add_rsqrt_fusion.1), kind=kOutput, calls=%fused_computation.35 | convolution fusion | flops 539033600 | bytes 5390848 | tf_op jit(solution)/shard_map/dot_general | solution.py:507
  11.3 3.0 %convolution_convert_fusion.12 = bf16[128,512]{1,0:T(8,128)(2,1)S(1)} fusion(bf16[4096,512]{1,0:T(8,128)(2,1)} %param.22, bf16[1,128,4096]{2,1,0:T(8,128)(2,1)S(1)} %copy-done.5, f32[4096]{0:T(1024)S(1)} %copy-done.39, f32[128]{0:T(128)S(1)} %add_rsqrt_fusion.1), kind=kOutput, calls=%fused_computation.37 | convolution fusion | flops 539033600 | bytes 5390848 | tf_op jit(solution)/shard_map/dot_general | solution.py:507
  14.6 2.9 %convolution_convert_fusion = bf16[128,4096]{1,0:T(8,128)(2,1)S(1)} fusion(bf16[128,512]{0,1:T(8,128)(2,1)S(1)} %bitcast.218, bf16[512,4096]{1,0:T(8,128)(2,1)} %param.24), kind=kOutput, calls=%fused_computation | convolution fusion | flops 537395200 | bytes 5373952 | tf_op jit(solution)/shard_map/dot_general | solution.py:514
  17.6 0.8 copy.177
  18.4 1.3 copy.178
  19.8 0.7 dynamic-slice_bitcast_fusion.cs
  20.5 1.3 dynamic_slice.30
  21.8 0.7 pad_maximum_fusion.1.kv
  22.5 0.7 pad_maximum_fusion.2.qo
  23.2 66.4 %gather_text.1 = (bf16[32,128,384]{2,1,0:T(8,128)(2,1)}, bf16[32,192,384]{2,1,0:T(8,128)(2,1)}, bf16[2,4,128,1024]{3,2,1,0:T(8,128)(2,1)}, f32[2,4,8,128]{3,2,1,0:T(8,128)}) custom-call(bf16[2,128,384]{2,1,0:T(8,128)(2,1)} %pad_maximum_fusion.1.kv, bf16[192,384]{1,0:T(8,128)(2,1)} %pad_maximum_fusion.2.qo, bf16[4,128,1024]{2,1,0:T(8,128)(2,1)} %bitcast.195, ...), custom_call_target="tpu_custom_call" | custom-call | tf_op jit(solution)/shard_map/gather_text/pallas_call | solution.py:519
  89.6 3.2 %copy.179 = bf16[2,128,4,1024]{3,2,1,0:T(4,128)(2,1)S(1)} copy(bf16[2,128,4,1024]{3,1,2,0:T(8,128)(2,1)} %bitcast.201) | data formatting | bytes 4194304 | tf_op jit(solution)/shard_map/transpose | solution.py:525
  92.8 0.9 copy.220
  93.7 0.8 slice_reduce_fusion.1
  94.7 1.3 fusion.9
  96.0 0.7 copy.228
  96.7 0.6 select_reduce_fusion.2
  97.3 0.7 select_reduce_fusion.4
  98.0 0.6 copy-done.31
  98.9 0.6 reshape.285.cap
  99.5 20.1 %spread_kv.1 = bf16[32,3,8,384]{3,2,1,0:T(8,128)(2,1)} custom-call(bf16[16,2,8,384]{3,2,1,0:T(8,128)(2,1)} %bitcast.208, s32[96]{0:T(128)} %reshape.285.cap), custom_call_target="tpu_custom_call" | custom-call | tf_op jit(solution)/shard_map/spread_kv/pallas_call | solution.py:529
  119.7 1.1 copy.227
  120.8 0.8 fusion.58
  121.9 4.5 %fusion.57 = (bf16[32,96,384]{2,1,0:T(8,128)(2,1)S(1)}, bf16[32,96,384]{2,1,0:T(8,128)(2,1)}) fusion(bf16[32,192,384]{2,1,0:T(8,128)(2,1)} %get-tuple-element.18), kind=kLoop, calls=%fused_computation.132 | loop fusion | bytes 9437184 | tf_op jit(solution)/shard_map/slice | solution.py:549
  126.7 0.6 fusion.3
  127.3 0.5 copy-done.1
  127.9 1.1 convolution_convert_fusion.8
  129.8 0.6 fusion.54
  131.4 1.5 reshape_squeeze.13
  132.9 2.9 %convolution_convert_fusion.7 = bf16[384,256]{1,0:T(8,128)(2,1)S(1)} fusion(bf16[3072,384]{1,0:T(8,128)(2,1)} %bitcast.186, bf16[256,3072]{1,0:T(8,128)(2,1)} %param.33), kind=kOutput, calls=%fused_computation.27 | convolution fusion | flops 604078080 | bytes 4128768 | tf_op jit(solution)/shard_map/dot_general | solution.py:483
  136.6 0.9 fusion.43
  137.5 1.1 copy.192
  138.6 0.7 copy-done.21
  139.3 1.1 fusion.12
  141.1 0.6 copy-done.23
  141.7 1.3 fusion.13
  143.7 0.9 copy.203
  144.6 0.5 fusion.10
  145.0 0.7 copy-done.17
  145.7 2.2 convolution_convert_fusion.3
  147.9 1.7 copy.199
  149.6 1.6 copy.200
  151.2 1.4 fusion.11
  152.6 0.7 copy-done.8
  153.3 3.9 %convolution_convert_fusion.4 = bf16[256,3072]{1,0:T(8,128)(2,1)} fusion(bf16[256,384]{0,1:T(8,128)(2,1)S(1)} %bitcast.203, bf16[3072,384]{1,0:T(8,128)(2,1)} %bitcast.187), kind=kOutput, calls=%fused_computation.8 | convolution fusion | flops 604766208 | bytes 4128768 | tf_op jit(solution)/shard_map/dot_general | solution.py:483
  157.2 1.7 copy.197
  158.9 1.6 copy.198
  160.5 2.6 %convolution_convert_fusion.2 = bf16[3072,384]{1,0:T(8,128)(2,1)} fusion(bf16[256,384]{0,1:T(8,128)(2,1)S(1)} %bitcast.212, bf16[256,3072]{1,0:T(8,128)(2,1)S(1)} %copy-done, f32[256]{0:T(256)S(1)} %add_rsqrt_fusion, f32[256]{0:T(256)S(1)} %broadcast_multiply_fusion.1), kind=kOutput, calls=%fused_computation.3 | convolution fusion | flops 608305152 | bytes 4130816 | tf_op jit(solution)/shard_map/dot_general | solution.py:483
  163.1 2.2 fusion
  165.3 4.4 %copy.196 = bf16[3072,384]{1,0:T(8,128)(2,1)} copy(bf16[3072,384]{0,1:T(8,128)(2,1)} %fusion) | data formatting | bytes 4718592 | tf_op jit(solution)/shard_map/convert_element_type | solution.py:569
  169.7 5.2 %pad_maximum_fusion.d_in = bf16[32,192,384]{2,1,0:T(8,128)(2,1)} fusion(bf16[32,96,384]{2,1,0:T(8,128)(2,1)} %bitcast.185, bf16[32,96,384]{2,1,0:T(8,128)(2,1)} %bitcast.200), kind=kLoop, calls=%fused_computation.1 | loop fusion | flops 9437184 | bytes 9437184 | tf_op jit(solution)/shard_map/concatenate | solution.py:569
  175.3 0.7 reshape.301.idx
  176.0 0.6 fusion.1
  176.6 1.7 copy-done.3
  178.2 1.0 constant_dynamic-slice_fusion.vhat
  179.2 53.5 %reduce_grads.1 = (f32[192,384]{1,0:T(8,128)}, f32[256,768]{1,0:T(8,128)}, f32[256,768]{1,0:T(8,128)}, f32[4,2,8,256]{3,2,1,0:T(8,128)}, bf16[32,8,384]{2,1,0:T(8,128)(2,1)}) custom-call(bf16[32,192,384]{2,1,0:T(8,128)(2,1)} %pad_maximum_fusion.d_in, bf16[4,256,768]{2,1,0:T(8,128)(2,1)} %bitcast.192, bf16[4,256,768]{2,1,0:T(8,128)(2,1)} %bitcast.191, ...), custom_call_target="tpu_custom_call" | custom-call | tf_op jit(solution)/shard_map/reduce_grads/pallas_call | solution.py:574
  232.7 1.0 slice_reduce_fusion
  233.7 2.4 add_convert_fusion
  236.1 0.9 add_convert_fusion.1
  236.9 0.7 slice_bitcast_fusion
  237.7 0.7 slice_bitcast_fusion.1
  (117 shorter events, 6.4 us)
Async XLA Ops:
  4.1 3.5 %copy-start.5 = (bf16[1,128,4096]{2,1,0:T(8,128)(2,1)S(1)}, bf16[1,128,4096]{2,1,0:T(8,128)(2,1)}, u32[]{:S(2)}) copy-start(bf16[1,128,4096]{2,1,0:T(8,128)(2,1)} %param.17) | copy-start | bytes 3145732
  4.1 3.5 %copy-start.39 = (f32[4096]{0:T(1024)S(1)}, f32[4096]{0:T(1024)}, u32[]{:S(2)}) copy-start(f32[4096]{0:T(1024)} %param.19) | copy-start | bytes 49156
  7.6 3.2 %copy-start.13 = (f32[8,128,128]{2,1,0:T(8,128)S(1)}, f32[8,128,128]{2,1,0:T(8,128)}, u32[]{:S(2)}) copy-start(f32[8,128,128]{2,1,0:T(8,128)} %param.23) | copy-start | bytes 1572868
  17.5 4.3 %copy-start.24 = (bf16[128,384]{1,0:T(8,128)(2,1)S(1)}, bf16[128,384]{1,0:T(8,128)(2,1)}, u32[]{:S(2)}) copy-start(bf16[128,384]{1,0:T(8,128)(2,1)} %param.27) | copy-start | bytes 294916
  17.5 4.2 %copy-start.25 = (bf16[128,384]{1,0:T(8,128)(2,1)S(1)}, bf16[128,384]{1,0:T(8,128)(2,1)}, u32[]{:S(2)}) copy-start(bf16[128,384]{1,0:T(8,128)(2,1)} %param.26) | copy-start | bytes 294916
  17.5 4.9 %copy-start.26 = (bf16[384,96]{0,1:T(8,128)(2,1)S(1)}, bf16[384,96]{0,1:T(8,128)(2,1)}, u32[]{:S(2)}) copy-start(bf16[384,96]{0,1:T(8,128)(2,1)} %param.32) | copy-start | bytes 221188
  17.5 4.9 %copy-start.27 = (bf16[96,384]{1,0:T(8,128)(2,1)S(1)}, bf16[96,384]{1,0:T(8,128)(2,1)}, u32[]{:S(2)}) copy-start(bf16[96,384]{1,0:T(8,128)(2,1)} %param.31) | copy-start | bytes 221188
  92.8 1.9 copy-start.38
  94.7 2.0 copy-start.30
  94.7 2.0 copy-start.36
  98.0 0.6 copy-start.31
  121.9 7.2 %copy-start.6 = (bf16[3,128,3,128]{1,3,0,2:T(8,128)(2,1)}, bf16[3,128,3,128]{1,3,0,2:T(8,128)(2,1)S(1)}, u32[]{:S(2)}) copy-start(bf16[3,128,3,128]{1,3,0,2:T(8,128)(2,1)S(1)} %copy.193) | copy-start | bytes 884740
  121.9 4.5 %copy-start = (bf16[256,3072]{1,0:T(8,128)(2,1)S(1)}, bf16[256,3072]{1,0:T(8,128)(2,1)}, u32[]{:S(2)}) copy-start(bf16[256,3072]{1,0:T(8,128)(2,1)} %param.28) | copy-start | bytes 4718596
  126.4 1.4 copy-start.1
  127.9 2.6 %copy-start.40 = (s32[32]{0:T(128)S(1)}, s32[32]{0:T(128)}, u32[]{:S(2)}) copy-start(s32[32]{0:T(128)} %param.18) | copy-start | bytes 388
  129.1 1.7 copy-start.10
  130.7 0.6 copy-start.14
  130.8 0.6 copy-start.28
  132.9 3.3 %copy-start.29 = (pred[256]{0:T(512)(128)(4,1)S(1)}, pred[256]{0:T(512)(128)(4,1)}, u32[]{:S(2)}) copy-start(pred[256]{0:T(512)(128)(4,1)} %copy-done.28) | copy-start | bytes 772
  135.8 1.7 copy-start.19
  135.9 0.8 copy-start.15
  136.6 2.7 %copy-start.11 = (bf16[256,384]{0,1:T(8,128)(2,1)S(1)}, bf16[256,384]{0,1:T(8,128)(2,1)}, u32[]{:S(2)}) copy-start(bf16[256,384]{0,1:T(8,128)(2,1)} %copy-done.10) | copy-start | bytes 589828
  137.5 4.2 %copy-start.35 = (bf16[3,256]{1,0:T(4,128)(2,1)S(1)}, bf16[3,256]{1,0:T(4,128)(2,1)}, u32[]{:S(2)}) copy-start(bf16[3,256]{1,0:T(4,128)(2,1)} %get-tuple-element.33) | copy-start | bytes 4612
  138.6 0.7 copy-start.21
  141.1 0.7 copy-start.23
  141.1 3.5 %copy-start.7 = (bf16[3,128,3,128]{1,3,0,2:T(8,128)(2,1)S(1)}, bf16[3,128,3,128]{1,3,0,2:T(8,128)(2,1)}, u32[]{:S(2)}) copy-start(bf16[3,128,3,128]{1,3,0,2:T(8,128)(2,1)} %copy-done.6) | copy-start | bytes 884740
  141.1 3.5 %copy-start.22 = (bf16[256,3,128]{2,0,1:T(8,128)(2,1)S(1)}, bf16[256,3,128]{2,0,1:T(8,128)(2,1)}, u32[]{:S(2)}) copy-start(bf16[256,3,128]{2,0,1:T(8,128)(2,1)} %copy-done.21) | copy-start | bytes 589828
  143.6 2.1 copy-start.2
  145.0 0.7 copy-start.17
  152.6 0.7 copy-start.8
  158.9 1.6 copy-start.18
  160.5 2.6 %copy-start.4 = (bf16[256,3072]{1,0:T(8,128)(2,1)S(1)}, bf16[256,3072]{1,0:T(8,128)(2,1)}, u32[]{:S(2)}) copy-start(bf16[256,3072]{1,0:T(8,128)(2,1)} %param.33) | copy-start | bytes 4718596
  160.5 2.6 %copy-start.9 = (bf16[3,128,256]{2,1,0:T(8,128)(2,1)S(1)}, bf16[3,128,256]{2,1,0:T(8,128)(2,1)}, u32[]{:S(2)}) copy-start(bf16[3,128,256]{2,1,0:T(8,128)(2,1)} %copy-done.8) | copy-start | bytes 589828
  169.7 5.2 %copy-start.34 = (s32[32]{0:T(128)S(1)}, s32[32]{0:T(128)}, u32[]{:S(2)}) copy-start(s32[32]{0:T(128)} %get-tuple-element.29) | copy-start | bytes 388
  169.7 5.2 %copy-start.37 = (s32[32]{0:T(128)S(1)}, s32[32]{0:T(128)}, u32[]{:S(2)}) copy-start(s32[32]{0:T(128)} %get-tuple-element.27) | copy-start | bytes 388
  169.7 5.3 %copy-start.32 = (s32[32]{0:T(128)S(1)}, s32[32]{0:T(128)}, u32[]{:S(2)}) copy-start(s32[32]{0:T(128)} %copy-done.31) | copy-start | bytes 388
  169.7 5.5 %copy-start.33 = (s32[32]{0:T(128)S(1)}, s32[32]{0:T(128)}, u32[]{:S(2)}) copy-start(s32[32]{0:T(128)} %get-tuple-element.26) | copy-start | bytes 388
  176.6 1.7 copy-start.3
  232.7 3.4 %copy-start.12 = (f32[256,768]{1,0:T(8,128)S(1)}, f32[256,768]{1,0:T(8,128)}, u32[]{:S(2)}) copy-start(f32[256,768]{1,0:T(8,128)} %get-tuple-element.19) | copy-start | bytes 2359300
  232.7 4.2 %copy-start.16 = (f32[192,384]{1,0:T(8,128)S(1)}, f32[192,384]{1,0:T(8,128)}, u32[]{:S(2)}) copy-start(f32[192,384]{1,0:T(8,128)} %get-tuple-element.22) | copy-start | bytes 884740
  232.7 5.0 %copy-start.20 = (bf16[32,8,384]{2,1,0:T(8,128)(2,1)S(1)}, bf16[32,8,384]{2,1,0:T(8,128)(2,1)}, u32[]{:S(2)}) copy-start(bf16[32,8,384]{2,1,0:T(8,128)(2,1)} %get-tuple-element.23) | copy-start | bytes 589828

commit v2 on v1

v2 whole, which is shorter than its diff:
```python
import math

import jax
import jax.numpy as jnp
from jax import lax
from jax.experimental import pallas as pl
from jax.experimental.pallas import tpu as pltpu
from jax.sharding import PartitionSpec as P
MESH = pl.DeviceIdType.MESH
BF, F32 = jnp.bfloat16, jnp.float32
DMA = pltpu.SemaphoreType.DMA
HEAD_SIZE = 128

class Links:
    def __init__(self, sems):
        self.sems, self.keys, self.pending = sems, {}, []
    def sem(self, key):
        return self.sems.at[self.keys.setdefault(key, len(self.keys))]
    def copy(self, src, dst, key, dev, group=None):
        send = self.sem(("s", group if group else key))
        return pltpu.make_async_remote_copy(src_ref=src, dst_ref=dst, send_sem=send, recv_sem=self.sem(("r", key)), device_id=dev, device_id_type=MESH)
    def send(self, src, dst, key, dev, group=None):
        c = self.copy(src, dst, key, dev, group)
        c.start()
        if group is None:
            self.pending.append(c)
    def recv(self, dst, key, dev, group=None):
        self.copy(dst, dst, key, dev, group).wait_recv()
    def sent(self, blocks, group, key, dev):
        self.copy(blocks, blocks, key, dev, group).wait_send()
    def drain(self):
        for c in self.pending:
            c.wait_send()
        self.pending = []

def place():
    g, f = lax.axis_index("grp"), lax.axis_index("fsdp")
    return dict(hi=g // 2, core=g % 2, y=f // 8, z=(f // 2) % 4, x=f % 2, g=g, f=f)

def dev(hi, core, y, z, x):
    return {"grp": hi * 2 + core, "fsdp": (y * 4 + z) * 2 + x}

class Gather:
    def __init__(self, L, me, name, G, rows):
        self.L, self.me, self.name, self.G, self.rows = L, me, name, G, rows
    def nb(self, part, first, d):
        m = self.me
        use_z = (m["x"] == 0) if (part == 0) == first else (m["x"] == 1)
        zi = jnp.where(use_z, (m["z"] + d) % 4, m["z"])
        yi = jnp.where(use_z, m["y"], (m["y"] + d) % 4)
        return {"fsdp": (yi * 4 + zi) * 2 + m["x"], "grp": m["g"]}
    def idx(self, part, d1, d2):
        m = self.me
        use_z = (m["x"] == 0) if part == 0 else (m["x"] == 1)
        dz = jnp.where(use_z, d1, d2)
        dy = jnp.where(use_z, d2, d1)
        px = m["x"] if part == 0 else 1 - m["x"]
        return (((m["y"] + dy) % 4) * 4 + (m["z"] + dz) % 4) * 2 + px
    def ref(self, part, d1, d2, half=None):
        b = self.G.at[self.idx(part, d1, d2)]
        if half is None:
            return b
        h = self.rows // 2
        return b.at[pl.ds(half * h, h)]
    def xsend(self, src):
        m = self.me
        self.L.send(src, self.G.at[m["f"]], (self.name, "x"), {"grp": m["g"], "fsdp": m["f"] + 1 - 2 * m["x"]}, self.name)
    def xrecv(self):
        m = self.me
        self.L.recv(self.ref(1, 0, 0), (self.name, "x"), {"grp": m["g"], "fsdp": m["f"] + 1 - 2 * m["x"]}, self.name)
    def s1(self, part, first, k, src=None):
        d = (0, 0) if first else (k, 0)
        r = self.ref(part, *d)
        src = r if src is None else src
        for s in (1, 3):
            self.L.send(src, r, (self.name, part, first, k, "s1", s), self.nb(part, first, s), self.name)
    def s2(self, part, first, k, s):
        o = 4 - s
        d = (o, 0) if first else (k, o)
        self.L.recv(self.ref(part, *d), (self.name, part, first, k, "s1", s), self.nb(part, first, o), self.name)
        half = 0 if s == 1 else 1
        r = self.ref(part, *d, half)
        self.L.send(r, r, (self.name, part, first, k, "s2", s), self.nb(part, first, s), self.name)
    def s3(self, part, first, k):
        d = (2, 0) if first else (k, 2)
        for s in (1, 3):
            half = 0 if s == 1 else 1
            self.L.recv(self.ref(part, *d, half), (self.name, part, first, k, "s2", s), self.nb(part, first, 4 - s), self.name)
    def run(self, own, xsrc):
        for st in self.stages(own, xsrc):
            st()
    def stages(self, own, xsrc):
        def a():
            self.s1(0, True, 0, own)
        def b():
            self.xrecv(); self.s1(1, True, 0)
        def c():
            self.s2(0, True, 0, 1); self.s2(0, True, 0, 3)
            self.s1(0, False, 0, own)
            self.s2(1, True, 0, 1); self.s2(1, True, 0, 3)
            self.s1(1, False, 0)
        def d():
            for k in (1, 3):
                self.s1(0, False, k); self.s1(1, False, k)
        def e():
            self.s3(0, True, 0); self.s1(0, False, 2)
            self.s3(1, True, 0); self.s1(1, False, 2)
        def fw(k):
            def f():
                for part in (0, 1):
                    self.s2(part, False, k, 1); self.s2(part, False, k, 3)
            return f
        def fin(k):
            def f():
                for part in (0, 1):
                    self.s3(part, False, k)
            return f
        return [a, b, c, d, e, fw(0), fw(1), fin(0), fw(3), fin(1), fw(2), fin(3), fin(2)]
    def sent(self):
        m = self.me
        self.L.sent(self.G.at[pl.ds(0, 31)], self.name, (self.name, "x"), {"grp": m["g"], "fsdp": m["f"] + 1 - 2 * m["x"]})

def barrier(me, devs):
    b = pltpu.get_barrier_semaphore()
    for d in devs:
        pl.semaphore_signal(b, inc=1, device_id=d, device_id_type=MESH)
    pl.semaphore_wait(b, len(devs))

def neighbours(me):
    m = me
    out = [{"grp": m["g"], "fsdp": m["f"] + 1 - 2 * m["x"]}]
    for d in (1, 3):
        out.append({"grp": m["g"], "fsdp": (m["y"] * 4 + (m["z"] + d) % 4) * 2 + m["x"]})
        out.append({"grp": m["g"], "fsdp": (((m["y"] + d) % 4) * 4 + m["z"]) * 2 + m["x"]})
    return out


class TwoStep:
    def __init__(self, L, me, name, parts, r0, r1, s1, r2):
        self.L, self.me, self.name = L, me, name
        self.parts, self.r, self.s1, self.r2 = parts, (r0, r1), s1, r2
        self.sib = {"grp": me["g"] + 1 - 2 * me["core"], "fsdp": me["f"]}
        self.opp = {"grp": (1 - me["hi"]) * 2 + me["core"], "fsdp": me["f"]}
    def order(self):
        hi, core = self.me["hi"], self.me["core"]
        return [2 * (1 - hi) + 1 - core, 2 * hi + 1 - core, 2 * (1 - hi) + core, 2 * hi + core]
    def start(self, j):
        self.L.send(self.parts.at[self.order()[j]], self.r[j], (self.name, "c", j), self.sib)
    def mid(self):
        m = self.me
        self.L.recv(self.r[0], (self.name, "c", 0), self.sib)
        for i in range(self.s1.shape[0] // 32):
            rows = pl.ds(i * 32, 32)
            self.s1[rows] = (self.parts[2 * (1 - m["hi"]) + m["core"], rows].astype(F32) + self.r[0][rows].astype(F32)).astype(BF)
        self.L.send(self.s1, self.r2, (self.name, "o"), self.opp)
    def end(self):
        self.L.recv(self.r[1], (self.name, "c", 1), self.sib)
        self.L.recv(self.r2, (self.name, "o"), self.opp)
    def total(self, rows):
        m = self.me
        return self.parts[2 * m["hi"] + m["core"], rows].astype(F32) + self.r[1][rows].astype(F32) + self.r2[rows].astype(F32)


def along_x(me, d):
    X = (me["hi"] * 2 + me["x"] + d) % 4
    return X // 2, X % 2


def same_core(me, d):
    hi, x = along_x(me, d)
    return dev(hi, me["core"], me["y"], me["z"], x)


class Eight:
    def __init__(self, L, me, name, E, rows):
        self.L, self.me, self.name, self.E, self.rows = L, me, name, E, rows
        self.sib = {"grp": me["g"] + 1 - 2 * me["core"], "fsdp": me["f"]}
    def ref(self, d, core, half=None):
        hi, x = along_x(self.me, d)
        r = self.E.at[x, hi * 2 + core]
        if half is None:
            return r
        h = self.rows // 2
        return r.at[pl.ds(half * h, h)]
    def start(self):
        r = self.ref(0, self.me["core"])
        for s in (1, 3):
            self.L.send(r, r, (self.name, "s1", s), same_core(self.me, s))
        self.L.send(r, r, (self.name, "sib", 0), self.sib)
    def mid(self):
        c = self.me["core"]
        for s in (1, 3):
            r = self.ref(4 - s, c)
            self.L.recv(r, (self.name, "s1", s), same_core(self.me, s))
            half = 0 if s == 1 else 1
            rh = self.ref(4 - s, c, half)
            self.L.send(rh, rh, (self.name, "s2", s), same_core(self.me, s))
            self.L.send(r, r, (self.name, "sib", 4 - s), self.sib)
    def mid2(self):
        c = self.me["core"]
        for s in (1, 3):
            half = 0 if s == 1 else 1
            rh = self.ref(2, c, half)
            self.L.recv(rh, (self.name, "s2", s), same_core(self.me, s))
            self.L.send(rh, rh, (self.name, "sib2", s), self.sib)
    def end(self):
        oc = 1 - self.me["core"]
        for d in (0, 1, 3):
            self.L.recv(self.ref(d, oc), (self.name, "sib", d), self.sib)
        for s in (1, 3):
            self.L.recv(self.ref(2, oc, 0 if s == 1 else 1), (self.name, "sib2", s), self.sib)


def eight_others(me):
    out = []
    for d in range(4):
        hi, x = along_x(me, d)
        for c in (0, 1):
            if d == 0 and c == 0:
                continue
            core = 1 - me["core"] if c == 1 else me["core"]
            out.append(((d, c), dev(hi, core, me["y"], me["z"], x), (x, hi * 2 + core)))
    return out


class Scatter:
    def __init__(self, L, me, name, D, ra, rb, rx):
        self.L, self.me, self.name, self.D, self.ra, self.rb, self.rx = L, me, name, D, ra, rb, rx
        self.rows = D.shape[1]
    def axis(self, part, stage):
        m = self.me
        own = m["x"] == 0 if part == 0 else m["x"] == 1
        return own if stage == 1 else jnp.logical_not(own)
    def nb(self, part, stage, d):
        m = self.me
        use_z = self.axis(part, stage)
        zi = jnp.where(use_z, (m["z"] + d) % 4, m["z"])
        yi = jnp.where(use_z, m["y"], (m["y"] + d) % 4)
        return {"fsdp": (yi * 4 + zi) * 2 + m["x"], "grp": m["g"]}
    def ref(self, part, stage, k, d, half=None):
        m = self.me
        use_z = self.axis(part, stage)
        dz = jnp.where(use_z, d, k)
        dy = jnp.where(use_z, k, d)
        px = m["x"] if part == 0 else 1 - m["x"]
        b = self.D.at[(((m["y"] + dy) % 4) * 4 + (m["z"] + dz) % 4) * 2 + px]
        if half is None:
            return b
        h = self.rows // 2
        return b.at[pl.ds(half * h, h)]
    def slot(self, stage, k):
        return k if stage == 0 else 4
    def far(self, part, stage, k):
        h = self.rows // 2
        for s in (1, 3):
            half = 0 if s == 1 else 1
            self.L.send(self.ref(part, stage, k, 2, half), self.ra.at[part, self.slot(stage, k), half], (self.name, part, stage, k, "far", s), self.nb(part, stage, s), self.name)
    def near(self, part, stage, k):
        h = self.rows // 2
        for s in (1, 3):
            half = 0 if s == 1 else 1
            buf = self.ra.at[part, self.slot(stage, k), half]
            self.L.recv(buf, (self.name, part, stage, k, "far", s), self.nb(part, stage, 4 - s), self.name)
            r = self.ref(part, stage, k, s, half)
            r[...] = (r[...].astype(F32) + buf[...].astype(F32)).astype(BF)
            self.L.send(self.ref(part, stage, k, s), self.rb.at[part, self.slot(stage, k), half], (self.name, part, stage, k, "near", s), self.nb(part, stage, s), self.name)
    def total(self, part, stage, k):
        for s in (1, 3):
            half = 0 if s == 1 else 1
            self.L.recv(self.rb.at[part, self.slot(stage, k), half], (self.name, part, stage, k, "near", s), self.nb(part, stage, 4 - s), self.name)
        b = self.rb.at[part, self.slot(stage, k)]
        return self.ref(part, stage, k, 0)[...].astype(F32) + b[0].astype(F32) + b[1].astype(F32)
    def fold(self, part, stage, k):
        t = self.total(part, stage, k)
        self.ref(part, stage, k, 0)[...] = t.astype(BF)
    def partner(self):
        m = self.me
        return {"grp": m["g"], "fsdp": m["f"] + 1 - 2 * m["x"]}
    def xsend(self):
        self.fold(1, 1, 0)
        self.L.send(self.ref(1, 1, 0, 0), self.rx, (self.name, "x"), self.partner(), self.name)
    def result(self):
        t = self.total(0, 1, 0)
        self.L.recv(self.rx, (self.name, "x"), self.partner(), self.name)
        return t + self.rx[...].astype(F32)
    def stages(self):
        def a():
            for k in (2, 1, 3, 0):
                for part in (1, 0):
                    self.far(part, 0, k)
        def b(k):
            def f():
                for part in (1, 0):
                    self.near(part, 0, k)
            return f
        def c(k):
            def f():
                for part in (1, 0):
                    self.fold(part, 0, k)
                    if k == 2:
                        self.far(part, 1, 0)
            return f
        def d():
            for part in (1, 0):
                self.near(part, 1, 0)
        return [a, b(2), b(1), c(2), b(3), c(1), b(0), c(3), d, c(0), self.xsend]
    def sent(self):
        self.L.sent(self.D.at[pl.ds(0, 31)], self.name, (self.name, "x"), self.partner())


def wait_bytes(like, send_sem, recv_sem, devid, recv=True, send=True):
    c = pltpu.make_async_remote_copy(src_ref=like, dst_ref=like, send_sem=send_sem, recv_sem=recv_sem, device_id=devid, device_id_type=MESH)
    if recv:
        c.wait_recv()
    if send:
        c.wait_send()


def dot(a, b, ca, cb):
    return lax.dot_general(a, b, (((ca,), (cb,)), ((), ())), preferred_element_type=F32)


class Refs:
    pass


P_IN = ["lens", "counts", "scap", "kv", "qo", "tgain", "fgain", "cs_h", "tq_h", "tk_h", "tv_h", "bias_h", "tout_h", "vid_h", "grad_h"]
P_OUT = {
    "qb": ((256, 384), BF),
    "da": ((256, 384), BF),
    "ks": ((2, 384, 384), BF),
    "gq": ((32, 192, 384), BF),
    "vnT": ((3072, 256), BF),
    "gradT": ((3072, 256), BF),
    "mu": ((256, 1), F32),
    "inv": ((256, 1), F32),
}
P_SCRATCH = {
    "cs": ((128, 4096), BF),
    "normed": ((128, 4096), BF),
    "wt": ((2, 4096, 512), BF),
    "bias": ((8, 128, 128), F32),
    "tqkv": ((3, 128, 512), BF),
    "tm": ((128, 512), BF),
    "vid": ((256, 3072), BF),
    "grad": ((256, 3072), BF),
    "vn": ((256, 3072), BF),
    "gw": ((32, 128, 384), BF),
    "parts": ((4, 128, 1024), BF),
    "t0": ((128, 1024), BF),
    "t1": ((128, 1024), BF),
    "t2": ((128, 1024), BF),
    "t3": ((128, 1024), BF),
    "E": ((2, 4, 128, 1024), BF),
    "sscol": ((128, 1), F32),
    "SS": ((2, 4, 8, 128), F32),
    "kvp": ((16, 2, 8, 384), BF),
    "C": ((32, 8, 384), BF),
    "sb": ((32, 3, 8, 384), BF),
    "R": ((32, 3, 8, 384), BF),
}
P_TABLES = {"end": 32, "first": 32, "cap": 96, "samp": 32}
Q_IN = ["edge", "sidx", "qb", "da", "ks", "mu", "inv", "gq_h", "vnT_h", "gradT_h", "vid_h", "grad_h"]
Q_OUT = {
    "updated": ((256, 768), BF),
    "igrad": ((256, 768), BF),
    "qgrad": ((96, 384), F32),
    "ograd": ((96, 384), F32),
    "kgrad": ((128, 384), BF),
    "vgrad": ((128, 384), BF),
}
Q_SCRATCH = {
    "gq": ((32, 192, 384), BF),
    "vnT": ((3072, 256), BF),
    "gradT": ((3072, 256), BF),
    "vid": ((256, 3072), BF),
    "grad": ((256, 3072), BF),
    "att": ((256, 384), BF),
    "dq": ((256, 384), BF),
    "w": ((3, 256, 128), F32),
    "mp": ((3, 256, 384), BF),
    "T": ((32, 3, 8, 384), BF),
    "Dw": ((32, 96, 384), BF),
    "Dq": ((32, 96, 384), BF),
    "ra1": ((2, 5, 2, 48, 384), BF),
    "rb1": ((2, 5, 2, 96, 384), BF),
    "rx1": ((96, 384), BF),
    "ra2": ((2, 5, 2, 48, 384), BF),
    "rb2": ((2, 5, 2, 96, 384), BF),
    "rx2": ((96, 384), BF),
    "op": ((4, 256, 768), BF),
    "o0": ((256, 768), BF),
    "o1": ((256, 768), BF),
    "o2": ((256, 768), BF),
    "o3": ((256, 768), BF),
    "dn": ((4, 256, 768), BF),
    "n0": ((256, 768), BF),
    "n1": ((256, 768), BF),
    "n2": ((256, 768), BF),
    "n3": ((256, 768), BF),
    "scol": ((2, 256, 1), F32),
    "stat": ((4, 2, 8, 256), F32),
    "RG": ((99, 8, 384), BF),
    "CG": ((32, 8, 384), BF),
    "KV": ((32, 8, 384), BF),
}


def fill_tables(r):
    def total(s, acc):
        acc = acc + r.counts[s]
        r.end[s] = acc
        return acc
    lax.fori_loop(0, 32, total, jnp.int32(0))

    @pl.loop(0, 32)
    def _(d):
        count = jnp.int32(0)
        for s in range(32):
            count = count + (r.end[s] <= 256 * d).astype(jnp.int32)
        r.first[d] = count
        for t in range(3):
            r.cap[d * 3 + t] = r.scap[jnp.minimum(count + t, 31)]

    @pl.loop(0, 32)
    def _(c):
        s = jnp.int32(0)
        for t in range(32):
            s = s + jnp.where(r.scap[t] == c, t, 0)
        s = jnp.minimum(s, 31)
        stop = r.end[s]
        d0 = (stop - r.counts[s]) // 256
        for m in range(5):
            d = d0 + m
            valid = (d < 32) & (d * 256 < stop)
            r.sidx[c * 5 + m] = jnp.clip(jnp.where(valid, 3 * d + s - r.first[jnp.minimum(d, 31)], 96), 0, 96)


def named(refs, names):
    r = Refs()
    for n, ref in zip(names, refs):
        setattr(r, n, ref)
    return r


def encode(*refs):
    r = named(refs, P_IN + list(P_OUT) + ["edge", "sidx"] + list(P_SCRATCH) + list(P_TABLES) + ["sems", "lsem", "asem"])
    me = place()
    f, g, core, hi = me["f"], me["g"], me["core"], me["hi"]
    L = Links(r.sems)
    loads = {}

    def load(name, src, dst):
        c = pltpu.make_async_copy(src, dst, r.lsem.at[len(loads)])
        c.start()
        loads[name] = c
    load("cs", r.cs_h, r.cs)

    def load_text(a, wh):
        for k in range(2):
            rows = pl.ds(k * 2048, 2048)
            load(("wt", a, k), wh.at[rows], r.wt.at[a % 2, rows])
    load_text(0, r.tq_h)
    load_text(1, r.tk_h)
    load("bias", r.bias_h, r.bias)
    load("vid", r.vid_h, r.vid)
    load("grad", r.grad_h, r.grad)

    others = eight_others(me)
    fs = [{"grp": g, "fsdp": (f + j) % 32} for j in range(1, 32)]
    barrier(me, fs + [{"grp": (g + j) % 4, "fsdp": f // 2 * 2 + x} for j in range(1, 4) for x in range(2)])

    A, B = Gather(L, me, "w", r.gw, 128), Gather(L, me, "q", r.gq, 192)
    sa, sb = A.stages(r.kv.at[me["x"]], None), B.stages(r.qo, None)
    A.xsend(r.kv.at[1 - me["x"]])
    B.xsend(r.qo)
    sa[0]()
    r.gw[f] = r.kv[me["x"]]
    r.gq[f] = r.qo[...]

    loads["cs"].wait()

    @pl.loop(0, 8)
    def _(i):
        rows = pl.ds(i * 16, 16)
        x = r.cs[rows].astype(F32)
        mean_square = jnp.mean(x * x, axis=-1, keepdims=True)
        r.normed[rows] = (x * lax.rsqrt(mean_square + 1e-06) * r.tgain[...]).astype(BF)

    def project(a):
        acc = jnp.zeros((128, 512), F32)
        for k in range(2):
            loads["wt", a, k].wait()
            acc = acc + jnp.dot(r.normed[:, pl.ds(k * 2048, 2048)], r.wt[a % 2, pl.ds(k * 2048, 2048)], preferred_element_type=F32)
        r.tqkv[a] = acc.astype(BF)
    sa[1]()
    project(0)
    load_text(2, r.tv_h)
    sa[2]()
    sa[3]()
    project(1)
    for k in range(8):
        load(("wo", k), r.tout_h.at[:, pl.ds(k * 512, 512)], r.wt.at[1, pl.ds(k * 512, 512)])
    sa[4]()
    sb[0]()
    project(2)
    sa[5]()
    sb[1]()
    loads["bias"].wait()
    lane = lax.broadcasted_iota(jnp.int32, (128, 128), 1)
    valid = lane < r.lens[f]

    def text_pair(p):
        cols = pl.ds(p * 128, 128)
        q, k, v = r.tqkv[0, :, cols], r.tqkv[1, :, cols], r.tqkv[2, :, cols]
        out = []
        for i in range(2):
            qh = jnp.where((lane < 64) == (i == 0), q.astype(F32), 0.0).astype(BF)
            ex = jnp.where(valid, jnp.exp(dot(qh, k, 1, 1) + r.bias[2 * p + i]), 0.0)
            wts = (ex / jnp.sum(ex, axis=-1, keepdims=True)).astype(BF)
            out.append(dot(wts, v, 1, 0))
        r.tm[:, cols] = jnp.where(lane < 64, out[0], out[1]).astype(BF)
    text_pair(0)
    text_pair(1)
    sa[6]()
    sb[2]()
    sb[3]()
    text_pair(2)
    text_pair(3)
    sa[7]()
    for k in range(8):
        loads["wo", k].wait()
    T = TwoStep(L, me, "t", r.parts, r.t0, r.t1, r.t2, r.t3)
    for j, s in enumerate(T.order()):
        for n in range(2):
            cols = pl.ds(n * 512, 512)
            r.parts[s, :, cols] = jnp.dot(r.tm[...], r.wt[1, pl.ds((2 * s + n) * 512, 512)], preferred_element_type=F32).astype(BF)
        if j < 2:
            T.start(j)
    sa[8]()
    sb[4]()
    T.mid()
    fill_tables(r)
    sa[9]()
    sa[10]()
    sb[5]()
    T.end()

    @pl.loop(0, 8)
    def _(i):
        rows, cols = pl.ds(i * 16, 16), pl.ds(pl.multiple_of(g * 1024, 1024), 1024)
        ts = T.total(rows) + r.cs[rows, cols].astype(F32)
        r.E[me["x"], g, rows] = (ts * r.fgain[:, cols]).astype(BF)
        r.sscol[rows] = jnp.sum(ts * ts, axis=1, keepdims=True)
    X = Eight(L, me, "e", r.E, 128)
    X.start()
    r.SS[me["x"], g] = jnp.broadcast_to(r.sscol[...], (128, 128)).T[:8]
    mine = r.SS.at[me["x"], g]
    for key, d, _ in others:
        L.send(mine, mine, ("ss", (4 - key[0]) % 4, key[1]), d)
    sb[6]()

    loads["vid"].wait()

    @pl.loop(0, 16)
    def _(i):
        rows = pl.ds(i * 16, 16)
        v = r.vid[rows].astype(F32)
        mean = jnp.mean(v, axis=-1, keepdims=True)
        center = v - mean
        inverse = lax.rsqrt(jnp.mean(center * center, axis=-1, keepdims=True) + 1e-06)
        r.mu[rows], r.inv[rows] = mean, inverse
        r.vn[rows] = (center * inverse).astype(BF)
    X.mid()
    sb[7]()
    loads["grad"].wait()

    @pl.loop(0, 24)
    def _(i):
        lanes = pl.ds(pl.multiple_of(i * 128, 128), 128)
        r.vnT[lanes] = r.vn[:, lanes].T
        r.gradT[lanes] = r.grad[:, lanes].T
    X.mid2()
    sa[11]()
    sa[12]()
    sb[8]()
    X.end()
    for key, d, slot in others:
        L.recv(r.SS.at[slot[0], slot[1]], ("ss", key[0], key[1]), d)

    acc = jnp.zeros((256, 384), F32)
    for k in range(4):
        acc = acc + jnp.dot(r.E[:, k].reshape(256, 1024), r.gw[k * 8 : k * 8 + 8].reshape(1024, 384), preferred_element_type=F32)
    for c in range(2):
        ss = r.SS[c, 0, :1] + r.SS[c, 1, :1] + r.SS[c, 2, :1] + r.SS[c, 3, :1]
        col = jnp.broadcast_to(ss, (128, 128)).T[:, :1]
        r.kvp[:, c] = (acc[c * 128 : c * 128 + 128] * lax.rsqrt(col / 4096 + 1e-06)).reshape(16, 8, 384).astype(BF)

    partner = {"grp": g, "fsdp": (f + 1) % 32}
    yz = f // 2

    @pl.loop(1, 16)
    def _(j):
        to = (yz + j) % 16
        pltpu.make_async_remote_copy(src_ref=r.kvp.at[to], dst_ref=r.C.at[pl.ds(2 * yz, 2)], send_sem=r.asem.at[0], recv_sem=r.asem.at[1], device_id={"grp": g, "fsdp": to * 2 + me["x"]}, device_id_type=MESH).start()
    r.C[pl.ds(2 * yz, 2)] = r.kvp[yz]
    sb[9]()
    wait_bytes(r.C.at[pl.ds(0, 30)], r.asem.at[0], r.asem.at[1], partner)

    @pl.loop(1, 32)
    def _(j):
        to = (f + j) % 32
        for s in range(3):
            r.sb[to, s] = r.C[r.cap[to * 3 + s]]
        pltpu.make_async_remote_copy(src_ref=r.sb.at[to], dst_ref=r.R.at[f], send_sem=r.asem.at[2], recv_sem=r.asem.at[3], device_id={"grp": g, "fsdp": to}, device_id_type=MESH).start()
    for s in range(3):
        r.R[f, s] = r.C[r.cap[f * 3 + s]]
    for s in sb[10:]:
        s()

    acc = jnp.zeros((256, 384), F32)
    acc2 = jnp.zeros((256, 384), F32)
    for k in range(4):
        cols = pl.ds(k * 768, 768)
        acc = acc + jnp.dot(r.vn[:, cols], r.gq[k * 8 : k * 8 + 8, 0:96].reshape(768, 384), preferred_element_type=F32)
    r.qb[...] = acc.astype(BF)
    for k in range(4):
        cols = pl.ds(k * 768, 768)
        acc2 = acc2 + jnp.dot(r.grad[:, cols], r.gq[k * 8 : k * 8 + 8, 96:192].reshape(768, 384), preferred_element_type=F32)
    r.da[...] = acc2.astype(BF)

    first = r.first[f]
    r.edge[0], r.edge[1] = r.end[jnp.minimum(first, 31)], r.end[jnp.minimum(first + 1, 31)]
    for s in range(3):
        r.edge[2 + s] = r.lens[r.cap[f * 3 + s]]
    wait_bytes(r.R.at[pl.ds(0, 31)], r.asem.at[2], r.asem.at[3], partner)
    for kv in range(2):
        for s in range(3):
            r.ks[kv, pl.ds(s * 128, 128)] = r.R[:, s].reshape(16, 2, 8, 384)[:, kv].astype(F32).reshape(128, 384).astype(BF)
    A.sent()
    B.sent()
    L.drain()


def attend(*refs):
    r = named(refs, Q_IN + list(Q_OUT) + list(Q_SCRATCH) + ["sems", "lsem", "asem"])
    me = place()
    f, g, core, hi = me["f"], me["g"], me["core"], me["hi"]
    L = Links(r.sems)
    partner = {"grp": g, "fsdp": (f + 1) % 32}
    loads = {}
    for i, n in enumerate(("gradT", "gq", "vnT", "vid", "grad")):
        loads[n] = pltpu.make_async_copy(getattr(r, n + "_h"), getattr(r, n), r.lsem.at[i])
        loads[n].start()
    barrier(me, [{"grp": g, "fsdp": (f + j) % 32} for j in range(1, 32)] + [{"grp": (g + j) % 4, "fsdp": f} for j in range(1, 4)])
    position = lax.broadcasted_iota(jnp.int32, (256, 128), 0) + f * 256
    slot = (position >= r.edge[0]).astype(jnp.int32) + (position >= r.edge[1]).astype(jnp.int32)
    token_len = jnp.where(slot == 0, r.edge[2], jnp.where(slot == 1, r.edge[3], r.edge[4]))
    token_valid = lax.broadcasted_iota(jnp.int32, (256, 128), 1) < token_len
    scale = 1.0 / math.sqrt(HEAD_SIZE)

    def pick(a):
        return jnp.where(slot == 0, a[:, 0:128], jnp.where(slot == 1, a[:, 128:256], a[:, 256:384]))

    def placed(a):
        return jnp.concatenate([jnp.where(slot == s, a, 0.0).astype(BF) for s in range(3)], axis=1)

    for h in range(3):
        cols = pl.ds(h * 128, 128)
        scores = pick(dot(r.qb[:, cols], r.ks[0, :, cols], 1, 1)) * scale
        ex = jnp.where(token_valid, jnp.exp(scores), 0.0)
        w = ex / jnp.sum(ex, axis=-1, keepdims=True)
        r.w[h] = w
        mp = placed(w)
        r.mp[h] = mp
        r.att[:, cols] = dot(mp, r.ks[1, :, cols], 1, 0).astype(BF)

    def weight_grad(D, left, right):
        @pl.loop(0, 8)
        def _(i):
            rows = pl.ds(i * 384, 384)
            D[pl.ds(i * 4, 4)] = dot(left[rows], right[...], 1, 0).reshape(4, 96, 384).astype(BF)
    loads["gradT"].wait()
    weight_grad(r.Dw, r.gradT, r.att)
    S1 = Scatter(L, me, "d1", r.Dw, r.ra1, r.rb1, r.rx1)
    S2 = Scatter(L, me, "d2", r.Dq, r.ra2, r.rb2, r.rx2)
    s1, s2 = S1.stages(), S2.stages()
    s1[0]()
    loads["gq"].wait()
    O = TwoStep(L, me, "o", r.op, r.o0, r.o1, r.o2, r.o3)
    N = TwoStep(L, me, "n", r.dn, r.n0, r.n1, r.n2, r.n3)
    for j, s in enumerate(O.order()):
        r.op[s] = dot(r.att[...], r.gq[pl.ds(s * 8, 8), 96:192].reshape(768, 384), 1, 1).astype(BF)
        if j < 2:
            O.start(j)
    s1[1]()

    for h in range(3):
        cols = pl.ds(h * 128, 128)
        d_probs = pick(dot(r.da[:, cols], r.ks[1, :, cols], 1, 1))
        w = r.w[h]
        ds = w * (d_probs - jnp.sum(w * d_probs, axis=-1, keepdims=True)) * scale
        ms = placed(ds)
        r.dq[:, cols] = dot(ms, r.ks[0, :, cols], 1, 0).astype(BF)
        kt = dot(ms, r.qb[:, cols], 0, 0)
        vt = dot(r.mp[h], r.da[:, cols], 0, 0)
        for s in range(3):
            rows = slice(s * 128, s * 128 + 128)
            both = jnp.stack([kt[rows].reshape(16, 8, 128), vt[rows].reshape(16, 8, 128)], axis=1)
            r.T[:, s, :, cols] = both.reshape(32, 8, 128).astype(BF)
    O.mid()

    @pl.loop(1, 32)
    def _(j):
        to = (f + j) % 32
        pltpu.make_async_remote_copy(src_ref=r.T.at[to], dst_ref=r.RG.at[pl.ds(3 * f, 3)], send_sem=r.asem.at[4], recv_sem=r.asem.at[5], device_id={"grp": g, "fsdp": to}, device_id_type=MESH).start()
    s1[2]()
    s1[3]()
    loads["vnT"].wait()
    weight_grad(r.Dq, r.vnT, r.dq)
    s2[0]()
    s1[4]()
    s1[5]()
    for j, s in enumerate(N.order()):
        r.dn[s] = dot(r.dq[...], r.gq[pl.ds(s * 8, 8), 0:96].reshape(768, 384), 1, 1).astype(BF)
        if j < 2:
            N.start(j)
    s1[6]()
    s1[7]()
    N.mid()
    s1[8]()
    s2[1]()
    s2[2]()
    r.RG[pl.ds(96, 3)] = jnp.zeros((3, 8, 384), BF)
    r.RG[pl.ds(3 * f, 3)] = r.T[f]
    wait_bytes(r.RG.at[pl.ds(0, 93)], r.asem.at[4], r.asem.at[5], partner)

    @pl.loop(0, 32)
    def _(c):
        acc = r.RG[r.sidx[c * 5]].astype(F32)
        for m in range(1, 5):
            acc = acc + r.RG[r.sidx[c * 5 + m]].astype(F32)
        r.CG[c] = acc.astype(BF)

    @pl.loop(1, 32)
    def _(j):
        to = (f + j) % 32
        pltpu.make_async_remote_copy(src_ref=r.CG.at[to], dst_ref=r.KV.at[f], send_sem=r.asem.at[6], recv_sem=r.asem.at[7], device_id={"grp": g, "fsdp": to}, device_id_type=MESH).start()
    r.KV[f] = r.CG[f]
    for i in (9, 10):
        s1[i]()
    for i in (3, 4, 5):
        s2[i]()
    O.end()
    loads["vid"].wait()
    loads["grad"].wait()
    cols = pl.ds(pl.multiple_of(g * 768, 768), 768)

    @pl.loop(0, 16)
    def _(i):
        rows = pl.ds(i * 16, 16)
        r.updated[rows] = (r.vid[rows, cols].astype(F32) + O.total(rows)).astype(BF)
    s2[6]()
    s2[7]()
    N.end()

    def video_hat(rows):
        return (r.vid[rows, cols].astype(F32) - r.mu[rows]) * r.inv[rows]

    @pl.loop(0, 16)
    def _(i):
        rows = pl.ds(i * 16, 16)
        t = N.total(rows)
        r.scol[0, rows] = jnp.sum(t, axis=1, keepdims=True)
        r.scol[1, rows] = jnp.sum(t * video_hat(rows), axis=1, keepdims=True)
    for k in range(2):
        r.stat[g, k] = jnp.broadcast_to(r.scol[k], (256, 128)).T[:8]
    grp = [{"grp": (g + j) % 4, "fsdp": f} for j in range(1, 4)]
    for j in range(1, 4):
        L.send(r.stat.at[g], r.stat.at[g], ("st", j), grp[j - 1])
    for i in (8, 9, 10):
        s2[i]()
    r.ograd[...] = S1.result()
    for j in range(1, 4):
        L.recv(r.stat.at[(g + 4 - j) % 4], ("st", j), grp[3 - j])
    for k in range(2):
        s = r.stat[0, k, :1] + r.stat[1, k, :1] + r.stat[2, k, :1] + r.stat[3, k, :1]
        r.scol[k] = jnp.broadcast_to(s / 3072, (128, 256)).T[:, :1]

    @pl.loop(0, 16)
    def _(i):
        rows = pl.ds(i * 16, 16)
        d = N.total(rows) - r.scol[0, rows] - video_hat(rows) * r.scol[1, rows]
        r.igrad[rows] = (r.grad[rows, cols].astype(F32) + r.inv[rows] * d).astype(BF)
    wait_bytes(r.KV.at[pl.ds(0, 31)], r.asem.at[6], r.asem.at[7], partner)
    r.kgrad[...] = r.KV[...].reshape(16, 2, 8, 384)[:, 0].astype(F32).reshape(128, 384).astype(BF)
    r.vgrad[...] = r.KV[...].reshape(16, 2, 8, 384)[:, 1].astype(F32).reshape(128, 384).astype(BF)
    r.qgrad[...] = S2.result()
    S1.sent()
    S2.sent()
    L.drain()


def local(caption_states, caption_lens, text_gain, text_query, text_key, text_value, text_bias, text_out, final_gain, cross_key, cross_value, video_states, video_counts, sample_caption, cross_query, cross_out, out_grad):
    kv = jnp.stack([cross_key, cross_value])
    qo = jnp.concatenate([cross_query, cross_out.T])
    V, M, A = pltpu.VMEM, pltpu.SMEM, pl.ANY

    def call(kernel, name, cid, args, spaces, outs, tables, scratch, smem):
        return pl.pallas_call(
            kernel,
            out_shape=tuple(jax.ShapeDtypeStruct(s, d) for s, d in outs.values()) + tuple(jax.ShapeDtypeStruct((n,), jnp.int32) for n in tables),
            in_specs=[pl.BlockSpec(memory_space=s) for s in spaces],
            out_specs=tuple(pl.BlockSpec(memory_space=V) for _ in outs) + tuple(pl.BlockSpec(memory_space=M) for _ in tables),
            scratch_shapes=[V(s, d) for s, d in scratch.values()] + [M((n,), jnp.int32) for n in smem] + [DMA((128,)), DMA((24,)), DMA((8,))],
            compiler_params=pltpu.CompilerParams(collective_id=cid, has_side_effects=True, vmem_limit_bytes=58 << 20),
            name=name,
        )(*args)
    args = [caption_lens, video_counts, sample_caption, kv, qo, text_gain[None], final_gain[None], caption_states.reshape(128, 4096), text_query, text_key, text_value, text_bias, text_out, video_states, out_grad]
    qb, da, ks, gq, vnT, gradT, mu, inv, edge, sidx = call(encode, "encode", 0, args, [M] * 3 + [V] * 4 + [A] * 8, P_OUT, (8, 160), P_SCRATCH, P_TABLES.values())
    args = [edge, sidx, qb, da, ks, mu, inv, gq, vnT, gradT, video_states, out_grad]
    updated, igrad, qgrad, ograd, kgrad, vgrad = call(attend, "attend", 1, args, [M] * 2 + [V] * 5 + [A] * 5, Q_OUT, (), Q_SCRATCH, ())
    return updated, igrad, qgrad, ograd.T, kgrad[None], vgrad[None]


def solution(mesh):
    in_specs = (P("fsdp"), P(), P(), P(None, "grp"), P(None, "grp"), P(None, "grp"), P("grp"), P("grp"), P(), P("fsdp", "grp"), P("fsdp", "grp"), P("fsdp"), P(), P(), P("fsdp", "grp"), P("grp", "fsdp"), P("fsdp"))
    out_specs = (P("fsdp", "grp"), P("fsdp", "grp"), P("fsdp", "grp"), P("grp", "fsdp"), P("fsdp", None, "grp"), P("fsdp", None, "grp"))
    return jax.shard_map(local, mesh=mesh, in_specs=in_specs, out_specs=out_specs, check_vma=False)
```

time: 242 us -> 153 us (0.63); the launches traced: 238 us -> 153 us
  local copies, waits for them, and re-layouts: 43.9 us -> 9.78 us
  matrix products: 33.9 us -> 0 us
  other arithmetic: 19.3 us -> 3.24 us
    dot_general x19 -> x0, matrix products: 33.9 us -> none  [the longest x5 13.8 us: dot(): lax.dot_general(a, b, (((ca,), (cb,)), ((), ())), preferred_element_type=...]
    convert_element_type x10 -> x0, local copies, waits for them, and re-layouts: 9.6 us -> none  [the longest x1 4.36 us: local(): dot(out_grad, att, 0, 0).astype(BF).reshape(32, 96, 384)]
    reshape x6 -> x0, local copies, waits for them, and re-layouts: 6.99 us -> none  [the longest x1 1.61 us: local(): dn = dot(dq, Wq, 1, 1).astype(BF).reshape(256, 4, 768).transpose(1, 0, 2)]
    reduce_sum x14 -> x0, other arithmetic: 6.53 us -> none  [the longest x1 1.52 us: rms_scale(): mean_square = jnp.mean(values * values, axis=-1, keepdims=True)]
    slice x4 -> x0, local copies, waits for them, and re-layouts: 5.3 us -> none  [the longest x1 4.49 us: local(): Wq, WoT = (gq[:, :96].reshape(3072, 384), gq[:, 96:].reshape(3072, 384))]
    concatenate x1 -> x0, other arithmetic: 5.22 us -> none  [local(): jnp.concatenate([dot(vn, dq, 0, 0).astype(BF).reshape(32, 96, 384), dot(o...]
    transpose x3 -> x0, local copies, waits for them, and re-layouts: 4.83 us -> none  [the longest x1 3.21 us: local(): X = E.transpose(0, 2, 1, 3).reshape(256, 4096)]
    dynamic_slice x5 -> x0, local copies, waits for them, and re-layouts: 4.44 us -> none  [the longest x1 1.28 us: local(): fg = lax.dynamic_slice_in_dim(final_gain, g * 1024, 1024, 0)[None]]
where the time goes in v2:
time: 153 us
  Pallas kernels  139 us (91%)
  local copies, waits for them, and re-layouts  9.78 us (6%)
  other arithmetic  3.24 us (2%)
    pallas_call x2, Pallas kernels, call(): pl.pallas_call(kernel, out_shape=tuple((jax.ShapeDtypeStruct(s, d) for s,...  139 us
    unnamed x6, local copies, waits for them, and re-layouts  9.78 us

profile of v2, /device:TPU:1, one launch (start us, length us, event | category | flops | bytes accessed | tf_op | source)
XLA Modules:
  0.0 152.5 jit_solution(1141446773615647132)
XLA Ops:
  0.6 1.6 %pad_maximum_fusion.1.refs_4_ = bf16[192,384]{1,0:T(8,128)(2,1)} fusion(bf16[96,384]{1,0:T(8,128)(2,1)} %bitcast.15, bf16[96,384]{1,0:T(8,128)(2,1)} %param.31), kind=kLoop, calls=%fused_computation.1 | loop fusion | flops 294912 | bytes 294912 | tf_op jit(solution)/shard_map/concatenate | solution.py:806
  2.2 1.6 %pad_maximum_fusion.refs_3_ = bf16[2,128,384]{2,1,0:T(8,128)(2,1)} fusion(bf16[1,128,384]{2,1,0:T(8,128)(2,1)} %bitcast.13, bf16[1,128,384]{2,1,0:T(8,128)(2,1)} %bitcast.14), kind=kLoop, calls=%fused_computation | loop fusion | flops 98304 | bytes 393216 | tf_op jit(solution)/shard_map/stack | solution.py:805
  3.9 85.1 %encode.1 = (bf16[256,384]{1,0:T(8,128)(2,1)}, bf16[256,384]{1,0:T(8,128)(2,1)}, bf16[2,384,384]{2,1,0:T(8,128)(2,1)}, bf16[32,192,384]{2,1,0:T(8,128)(2,1)}, bf...) custom-call(s32[32]{0:T(128)} %refs_0_.1, ...), custom_call_target="tpu_custom_call" | custom-call | tf_op jit(solution)/shard_map/encode/pallas_call | solution.py:810
  89.0 53.7 %attend.1 = (bf16[256,768]{1,0:T(8,128)(2,1)}, bf16[256,768]{1,0:T(8,128)(2,1)}, f32[96,384]{1,0:T(8,128)}, f32[96,384]{1,0:T(8,128)}, bf16[128,384]{1,0:T(8,128)(2,1)}, /*index=5*/bf16[128,384]{1,0:T(8,128)(2,1)}) custom-call(s32[8]{0:T(128)} %get-tuple-element.22.refs_0_, s32[160]{0:T(256)} %get-tuple-element.23.refs_1_, ...), custom_call_target="tpu_custom_call" | custom-call | tf_op jit(solution)/shard_map/attend/pallas_call | solution.py:810
  142.8 1.8 %copy.29 = bf16[256,768]{1,0:T(8,128)(2,1)} copy(bf16[256,768]{1,0:T(8,128)(2,1)} %get-tuple-element.44) | data formatting | bytes 786432
  144.5 1.8 %copy.30 = bf16[256,768]{1,0:T(8,128)(2,1)} copy(bf16[256,768]{1,0:T(8,128)(2,1)} %get-tuple-element.45) | data formatting | bytes 786432
  146.3 1.6 %copy.31 = f32[96,384]{1,0:T(8,128)} copy(f32[96,384]{1,0:T(8,128)} %get-tuple-element.46) | data formatting | bytes 294912
  147.9 1.6 %copy.32 = f32[384,96]{0,1:T(8,128)} copy(f32[384,96]{0,1:T(8,128)} %bitcast.10) | data formatting | bytes 294912
  149.5 1.5 %copy.33 = bf16[1,128,384]{2,1,0:T(8,128)(2,1)} copy(bf16[1,128,384]{2,1,0:T(8,128)(2,1)} %bitcast.12) | data formatting | bytes 196608
  151.0 1.5 %copy.34 = bf16[1,128,384]{2,1,0:T(8,128)(2,1)} copy(bf16[1,128,384]{2,1,0:T(8,128)(2,1)} %bitcast.11) | data formatting | bytes 196608

commit v3 on v2

--- a/solution.py
+++ b/solution.py
@@ -86,19 +86,18 @@
         for s in (1, 3):
             half = 0 if s == 1 else 1
             self.L.recv(self.ref(part, *d, half), (self.name, part, first, k, "s2", s), self.nb(part, first, 4 - s), self.name)
-    def run(self, own, xsrc):
-        for st in self.stages(own, xsrc):
-            st()
-    def stages(self, own, xsrc):
+    def stages(self, own):
         def a():
             self.s1(0, True, 0, own)
+            self.s1(0, False, 0, own)
         def b():
-            self.xrecv(); self.s1(1, True, 0)
+            self.xrecv()
+            self.s1(1, True, 0)
+            self.s1(1, False, 0)
         def c():
-            self.s2(0, True, 0, 1); self.s2(0, True, 0, 3)
-            self.s1(0, False, 0, own)
-            self.s2(1, True, 0, 1); self.s2(1, True, 0, 3)
-            self.s1(1, False, 0)
+            for part in (0, 1):
+                self.s2(part, True, 0, 1)
+                self.s2(part, True, 0, 3)
         def d():
             for k in (1, 3):
                 self.s1(0, False, k); self.s1(1, False, k)
@@ -324,7 +323,7 @@
     pass
 
 
-P_IN = ["lens", "counts", "scap", "kv", "qo", "tgain", "fgain", "cs_h", "tq_h", "tk_h", "tv_h", "bias_h", "tout_h", "vid_h", "grad_h"]
+P_IN = ["lens", "counts", "scap", "tgain", "fgain", "cs_h", "tq_h", "tk_h", "tv_h", "bias_h", "tout_h", "vid_h", "grad_h", "ck_h", "cv_h", "cq_h", "co_h"]
 P_OUT = {
     "qb": ((256, 384), BF),
     "da": ((256, 384), BF),
@@ -336,6 +335,8 @@
     "inv": ((256, 1), F32),
 }
 P_SCRATCH = {
+    "kv": ((2, 128, 384), BF),
+    "qo": ((192, 384), BF),
     "cs": ((128, 4096), BF),
     "normed": ((128, 4096), BF),
     "wt": ((2, 4096, 512), BF),
@@ -454,6 +455,10 @@
         c = pltpu.make_async_copy(src, dst, r.lsem.at[len(loads)])
         c.start()
         loads[name] = c
+    load("ck", r.ck_h, r.kv.at[0])
+    load("cv", r.cv_h, r.kv.at[1])
+    load("cq", r.cq_h, r.qo.at[pl.ds(0, 96)])
+    load("co", r.co_h, r.qo.at[pl.ds(96, 96)])
     load("cs", r.cs_h, r.cs)
 
     def load_text(a, wh):
@@ -471,10 +476,13 @@
     barrier(me, fs + [{"grp": (g + j) % 4, "fsdp": f // 2 * 2 + x} for j in range(1, 4) for x in range(2)])
 
     A, B = Gather(L, me, "w", r.gw, 128), Gather(L, me, "q", r.gq, 192)
-    sa, sb = A.stages(r.kv.at[me["x"]], None), B.stages(r.qo, None)
+    sa, sb = A.stages(r.kv.at[me["x"]]), B.stages(r.qo)
+    for n in ("ck", "cv", "cq", "co"):
+        loads[n].wait()
     A.xsend(r.kv.at[1 - me["x"]])
+    sa[0]()
     B.xsend(r.qo)
-    sa[0]()
+    sb[0]()
     r.gw[f] = r.kv[me["x"]]
     r.gq[f] = r.qo[...]
 
@@ -493,19 +501,16 @@
             loads["wt", a, k].wait()
             acc = acc + jnp.dot(r.normed[:, pl.ds(k * 2048, 2048)], r.wt[a % 2, pl.ds(k * 2048, 2048)], preferred_element_type=F32)
         r.tqkv[a] = acc.astype(BF)
-    sa[1]()
     project(0)
     load_text(2, r.tv_h)
-    sa[2]()
-    sa[3]()
+    sa[1]()
     project(1)
     for k in range(8):
         load(("wo", k), r.tout_h.at[:, pl.ds(k * 512, 512)], r.wt.at[1, pl.ds(k * 512, 512)])
-    sa[4]()
-    sb[0]()
+    sb[1]()
     project(2)
-    sa[5]()
-    sb[1]()
+    sa[2]()
+    sa[3]()
     loads["bias"].wait()
     lane = lax.broadcasted_iota(jnp.int32, (128, 128), 1)
     valid = lane < r.lens[f]
@@ -522,12 +527,12 @@
         r.tm[:, cols] = jnp.where(lane < 64, out[0], out[1]).astype(BF)
     text_pair(0)
     text_pair(1)
-    sa[6]()
     sb[2]()
     sb[3]()
     text_pair(2)
     text_pair(3)
-    sa[7]()
+    sa[4]()
+    sa[5]()
     for k in range(8):
         loads["wo", k].wait()
     T = TwoStep(L, me, "t", r.parts, r.t0, r.t1, r.t2, r.t3)
@@ -537,13 +542,12 @@
             r.parts[s, :, cols] = jnp.dot(r.tm[...], r.wt[1, pl.ds((2 * s + n) * 512, 512)], preferred_element_type=F32).astype(BF)
         if j < 2:
             T.start(j)
-    sa[8]()
     sb[4]()
+    sb[5]()
     T.mid()
     fill_tables(r)
-    sa[9]()
-    sa[10]()
-    sb[5]()
+    sa[6]()
+    sb[6]()
     T.end()
 
     @pl.loop(0, 8)
@@ -558,7 +562,8 @@
     mine = r.SS.at[me["x"], g]
     for key, d, _ in others:
         L.send(mine, mine, ("ss", (4 - key[0]) % 4, key[1]), d)
-    sb[6]()
+    sa[7]()
+    sa[8]()
 
     loads["vid"].wait()
 
@@ -573,6 +578,7 @@
         r.vn[rows] = (center * inverse).astype(BF)
     X.mid()
     sb[7]()
+    sb[8]()
     loads["grad"].wait()
 
     @pl.loop(0, 24)
@@ -581,9 +587,10 @@
         r.vnT[lanes] = r.vn[:, lanes].T
         r.gradT[lanes] = r.grad[:, lanes].T
     X.mid2()
-    sa[11]()
-    sa[12]()
-    sb[8]()
+    for i in range(9, 13):
+        sa[i]()
+    sb[9]()
+    sb[10]()
     X.end()
     for key, d, slot in others:
         L.recv(r.SS.at[slot[0], slot[1]], ("ss", key[0], key[1]), d)
@@ -604,7 +611,6 @@
         to = (yz + j) % 16
         pltpu.make_async_remote_copy(src_ref=r.kvp.at[to], dst_ref=r.C.at[pl.ds(2 * yz, 2)], send_sem=r.asem.at[0], recv_sem=r.asem.at[1], device_id={"grp": g, "fsdp": to * 2 + me["x"]}, device_id_type=MESH).start()
     r.C[pl.ds(2 * yz, 2)] = r.kvp[yz]
-    sb[9]()
     wait_bytes(r.C.at[pl.ds(0, 30)], r.asem.at[0], r.asem.at[1], partner)
 
     @pl.loop(1, 32)
@@ -615,7 +621,7 @@
         pltpu.make_async_remote_copy(src_ref=r.sb.at[to], dst_ref=r.R.at[f], send_sem=r.asem.at[2], recv_sem=r.asem.at[3], device_id={"grp": g, "fsdp": to}, device_id_type=MESH).start()
     for s in range(3):
         r.R[f, s] = r.C[r.cap[f * 3 + s]]
-    for s in sb[10:]:
+    for s in sb[11:]:
         s()
 
     acc = jnp.zeros((256, 384), F32)
@@ -801,9 +807,15 @@
     L.drain()
 
 
+def hand_over(*refs):
+    copies = [pltpu.make_async_copy(refs[i], refs[6 + i], refs[12].at[i]) for i in range(6)]
+    for c in copies:
+        c.start()
+    for c in copies:
+        c.wait()
+
+
 def local(caption_states, caption_lens, text_gain, text_query, text_key, text_value, text_bias, text_out, final_gain, cross_key, cross_value, video_states, video_counts, sample_caption, cross_query, cross_out, out_grad):
-    kv = jnp.stack([cross_key, cross_value])
-    qo = jnp.concatenate([cross_query, cross_out.T])
     V, M, A = pltpu.VMEM, pltpu.SMEM, pl.ANY
 
     def call(kernel, name, cid, args, spaces, outs, tables, scratch, smem):
@@ -816,10 +828,18 @@
             compiler_params=pltpu.CompilerParams(collective_id=cid, has_side_effects=True, vmem_limit_bytes=58 << 20),
             name=name,
         )(*args)
-    args = [caption_lens, video_counts, sample_caption, kv, qo, text_gain[None], final_gain[None], caption_states.reshape(128, 4096), text_query, text_key, text_value, text_bias, text_out, video_states, out_grad]
-    qb, da, ks, gq, vnT, gradT, mu, inv, edge, sidx = call(encode, "encode", 0, args, [M] * 3 + [V] * 4 + [A] * 8, P_OUT, (8, 160), P_SCRATCH, P_TABLES.values())
+    args = [caption_lens, video_counts, sample_caption, text_gain[None], final_gain[None], caption_states.reshape(128, 4096), text_query, text_key, text_value, text_bias, text_out, video_states, out_grad, cross_key, cross_value, cross_query, cross_out.T]
+    qb, da, ks, gq, vnT, gradT, mu, inv, edge, sidx = call(encode, "encode", 0, args, [M] * 3 + [V] * 2 + [A] * 12, P_OUT, (8, 160), P_SCRATCH, P_TABLES.values())
     args = [edge, sidx, qb, da, ks, mu, inv, gq, vnT, gradT, video_states, out_grad]
-    updated, igrad, qgrad, ograd, kgrad, vgrad = call(attend, "attend", 1, args, [M] * 2 + [V] * 5 + [A] * 5, Q_OUT, (), Q_SCRATCH, ())
+    outs = call(attend, "attend", 1, args, [M] * 2 + [V] * 5 + [A] * 5, Q_OUT, (), Q_SCRATCH, ())
+    updated, igrad, qgrad, ograd, kgrad, vgrad = pl.pallas_call(
+        hand_over,
+        out_shape=tuple(jax.ShapeDtypeStruct(s, d) for s, d in Q_OUT.values()),
+        in_specs=[pl.BlockSpec(memory_space=A)] * 6,
+        out_specs=(pl.BlockSpec(memory_space=A),) * 6,
+        scratch_shapes=[DMA((6,))],
+        name="hand_over",
+    )(*outs)
     return updated, igrad, qgrad, ograd.T, kgrad[None], vgrad[None]
 
 

time: 153 us -> 167 us (1.092)
  Pallas kernels: 139 us -> 166 us
  local copies, waits for them, and re-layouts: 9.78 us -> 0 us
  other arithmetic: 3.24 us -> 0 us
    pallas_call x0 -> x1, Pallas kernels: none -> 39.9 us  [local(): pl.pallas_call(hand_over, out_shape=tuple((jax.ShapeDtypeStruct(s, d) for...]
    pallas_call x2, Pallas kernels: 139 us -> 126 us  [call(): pl.pallas_call(kernel, out_shape=tuple((jax.ShapeDtypeStruct(s, d) for s,...]
    unnamed x6 -> x0, local copies, waits for them, and re-layouts: 9.78 us -> none
where the time goes in v3:
time: 167 us
  Pallas kernels  166 us (99%)
    pallas_call x2, Pallas kernels, call(): pl.pallas_call(kernel, out_shape=tuple((jax.ShapeDtypeStruct(s, d) for s,...  126 us
    pallas_call x1, Pallas kernels, local(): pl.pallas_call(hand_over, out_shape=tuple((jax.ShapeDtypeStruct(s, d) for...  39.9 us

profile of v3, /device:TPU:1, one launch (start us, length us, event | category | flops | bytes accessed | tf_op | source)
XLA Modules:
  0.0 166.8 jit_solution(3964982352076752478)
XLA Ops:
  0.6 67.4 %encode.1 = (bf16[256,384]{1,0:T(8,128)(2,1)}, bf16[256,384]{1,0:T(8,128)(2,1)}, bf16[2,384,384]{2,1,0:T(8,128)(2,1)}, bf16[32,192,384]{2,1,0:T(8,128)(2,1)}, bf...) custom-call(s32[32]{0:T(128)} %refs_0_.1, ...), custom_call_target="tpu_custom_call" | custom-call | tf_op jit(solution)/shard_map/encode/pallas_call | solution.py:822
  68.1 58.7 %attend.1 = (bf16[256,768]{1,0:T(8,128)(2,1)}, bf16[256,768]{1,0:T(8,128)(2,1)}, f32[96,384]{1,0:T(8,128)}, f32[96,384]{1,0:T(8,128)}, bf16[128,384]{1,0:T(8,128)(2,1)}, /*index=5*/bf16[128,384]{1,0:T(8,128)(2,1)}) custom-call(s32[8]{0:T(128)} %get-tuple-element.28.refs_0_, s32[160]{0:T(256)} %get-tuple-element.29.refs_1_, ...), custom_call_target="tpu_custom_call" | custom-call | tf_op jit(solution)/shard_map/attend/pallas_call | solution.py:822
  126.8 39.9 %hand_over.1 = (bf16[256,768]{1,0:T(8,128)(2,1)}, bf16[256,768]{1,0:T(8,128)(2,1)}, f32[96,384]{1,0:T(8,128)}, f32[96,384]{1,0:T(8,128)}, bf16[128,384]{1,0:T(8,128)(2,1)}, /*index=5*/bf16[128,384]{1,0:T(8,128)(2,1)}) custom-call(bf16[256,768]{1,0:T(8,128)(2,1)} %get-tuple-element.38.refs_0_, bf16[256,768]{1,0:T(8,128)(2,1)} %get-tuple-element.39.refs_1_, ...), custom_call_target="tpu_custom_call" | custom-call | tf_op jit(solution)/shard_map/hand_over/pallas_call | solution.py:835

commit v4 on v3

--- a/solution.py
+++ b/solution.py
@@ -328,11 +328,13 @@
     "qb": ((256, 384), BF),
     "da": ((256, 384), BF),
     "ks": ((2, 384, 384), BF),
+    "mu": ((256, 1), F32),
+    "inv": ((256, 1), F32),
+}
+P_FAR = {
     "gq": ((32, 192, 384), BF),
     "vnT": ((3072, 256), BF),
     "gradT": ((3072, 256), BF),
-    "mu": ((256, 1), F32),
-    "inv": ((256, 1), F32),
 }
 P_SCRATCH = {
     "kv": ((2, 128, 384), BF),
@@ -380,6 +382,7 @@
     "dq": ((256, 384), BF),
     "w": ((3, 256, 128), F32),
     "mp": ((3, 256, 384), BF),
+    "ms": ((3, 256, 384), BF),
     "T": ((32, 3, 8, 384), BF),
     "Dw": ((32, 96, 384), BF),
     "Dq": ((32, 96, 384), BF),
@@ -445,7 +448,7 @@
 
 
 def encode(*refs):
-    r = named(refs, P_IN + list(P_OUT) + ["edge", "sidx"] + list(P_SCRATCH) + list(P_TABLES) + ["sems", "lsem", "asem"])
+    r = named(refs, P_IN + list(P_OUT) + [n + "_o" for n in P_FAR] + ["edge", "sidx"] + list(P_FAR) + list(P_SCRATCH) + list(P_TABLES) + ["sems", "lsem", "asem"])
     me = place()
     f, g, core, hi = me["f"], me["g"], me["core"], me["hi"]
     L = Links(r.sems)
@@ -586,6 +589,8 @@
         lanes = pl.ds(pl.multiple_of(i * 128, 128), 128)
         r.vnT[lanes] = r.vn[:, lanes].T
         r.gradT[lanes] = r.grad[:, lanes].T
+    load("vnT_o", r.vnT, r.vnT_o)
+    load("gradT_o", r.gradT, r.gradT_o)
     X.mid2()
     for i in range(9, 13):
         sa[i]()
@@ -623,6 +628,7 @@
         r.R[f, s] = r.C[r.cap[f * 3 + s]]
     for s in sb[11:]:
         s()
+    load("gq_o", r.gq, r.gq_o)
 
     acc = jnp.zeros((256, 384), F32)
     acc2 = jnp.zeros((256, 384), F32)
@@ -646,6 +652,8 @@
     A.sent()
     B.sent()
     L.drain()
+    for n in P_FAR:
+        loads[n + "_o"].wait()
 
 
 def attend(*refs):
@@ -707,36 +715,38 @@
         w = r.w[h]
         ds = w * (d_probs - jnp.sum(w * d_probs, axis=-1, keepdims=True)) * scale
         ms = placed(ds)
+        r.ms[h] = ms
         r.dq[:, cols] = dot(ms, r.ks[0, :, cols], 1, 0).astype(BF)
-        kt = dot(ms, r.qb[:, cols], 0, 0)
+    O.mid()
+    loads["vnT"].wait()
+    weight_grad(r.Dq, r.vnT, r.dq)
+    s2[0]()
+    s1[2]()
+    s1[3]()
+    for j, s in enumerate(N.order()):
+        r.dn[s] = dot(r.dq[...], r.gq[pl.ds(s * 8, 8), 0:96].reshape(768, 384), 1, 1).astype(BF)
+        if j < 2:
+            N.start(j)
+    for h in range(3):
+        cols = pl.ds(h * 128, 128)
+        kt = dot(r.ms[h], r.qb[:, cols], 0, 0)
         vt = dot(r.mp[h], r.da[:, cols], 0, 0)
         for s in range(3):
             rows = slice(s * 128, s * 128 + 128)
             both = jnp.stack([kt[rows].reshape(16, 8, 128), vt[rows].reshape(16, 8, 128)], axis=1)
             r.T[:, s, :, cols] = both.reshape(32, 8, 128).astype(BF)
-    O.mid()
 
     @pl.loop(1, 32)
     def _(j):
         to = (f + j) % 32
         pltpu.make_async_remote_copy(src_ref=r.T.at[to], dst_ref=r.RG.at[pl.ds(3 * f, 3)], send_sem=r.asem.at[4], recv_sem=r.asem.at[5], device_id={"grp": g, "fsdp": to}, device_id_type=MESH).start()
-    s1[2]()
-    s1[3]()
-    loads["vnT"].wait()
-    weight_grad(r.Dq, r.vnT, r.dq)
-    s2[0]()
-    s1[4]()
-    s1[5]()
-    for j, s in enumerate(N.order()):
-        r.dn[s] = dot(r.dq[...], r.gq[pl.ds(s * 8, 8), 0:96].reshape(768, 384), 1, 1).astype(BF)
-        if j < 2:
-            N.start(j)
-    s1[6]()
-    s1[7]()
     N.mid()
-    s1[8]()
+    for i in range(4, 8):
+        s1[i]()
     s2[1]()
     s2[2]()
+    s1[8]()
+    s2[3]()
     r.RG[pl.ds(96, 3)] = jnp.zeros((3, 8, 384), BF)
     r.RG[pl.ds(3 * f, 3)] = r.T[f]
     wait_bytes(r.RG.at[pl.ds(0, 93)], r.asem.at[4], r.asem.at[5], partner)
@@ -755,7 +765,7 @@
     r.KV[f] = r.CG[f]
     for i in (9, 10):
         s1[i]()
-    for i in (3, 4, 5):
+    for i in (4, 5):
         s2[i]()
     O.end()
     loads["vid"].wait()
@@ -808,36 +818,41 @@
 
 
 def hand_over(*refs):
-    copies = [pltpu.make_async_copy(refs[i], refs[6 + i], refs[12].at[i]) for i in range(6)]
-    for c in copies:
+    held, sem = refs[12:18], refs[18]
+    into = [pltpu.make_async_copy(refs[i], held[i], sem.at[i]) for i in range(6)]
+    out = [pltpu.make_async_copy(held[i], refs[6 + i], sem.at[6 + i]) for i in range(6)]
+    for c in into:
         c.start()
-    for c in copies:
+    for i in range(6):
+        into[i].wait()
+        out[i].start()
+    for c in out:
         c.wait()
 
 
 def local(caption_states, caption_lens, text_gain, text_query, text_key, text_value, text_bias, text_out, final_gain, cross_key, cross_value, video_states, video_counts, sample_caption, cross_query, cross_out, out_grad):
     V, M, A = pltpu.VMEM, pltpu.SMEM, pl.ANY
 
-    def call(kernel, name, cid, args, spaces, outs, tables, scratch, smem):
+    def call(kernel, name, cid, args, spaces, outs, far, tables, scratch, smem):
         return pl.pallas_call(
             kernel,
-            out_shape=tuple(jax.ShapeDtypeStruct(s, d) for s, d in outs.values()) + tuple(jax.ShapeDtypeStruct((n,), jnp.int32) for n in tables),
+            out_shape=tuple(jax.ShapeDtypeStruct(s, d) for s, d in (outs | far).values()) + tuple(jax.ShapeDtypeStruct((n,), jnp.int32) for n in tables),
             in_specs=[pl.BlockSpec(memory_space=s) for s in spaces],
-            out_specs=tuple(pl.BlockSpec(memory_space=V) for _ in outs) + tuple(pl.BlockSpec(memory_space=M) for _ in tables),
-            scratch_shapes=[V(s, d) for s, d in scratch.values()] + [M((n,), jnp.int32) for n in smem] + [DMA((128,)), DMA((24,)), DMA((8,))],
+            out_specs=tuple(pl.BlockSpec(memory_space=V) for _ in outs) + tuple(pl.BlockSpec(memory_space=A) for _ in far) + tuple(pl.BlockSpec(memory_space=M) for _ in tables),
+            scratch_shapes=[V(s, d) for s, d in (far | scratch).values()] + [M((n,), jnp.int32) for n in smem] + [DMA((128,)), DMA((32,)), DMA((8,))],
             compiler_params=pltpu.CompilerParams(collective_id=cid, has_side_effects=True, vmem_limit_bytes=58 << 20),
             name=name,
         )(*args)
     args = [caption_lens, video_counts, sample_caption, text_gain[None], final_gain[None], caption_states.reshape(128, 4096), text_query, text_key, text_value, text_bias, text_out, video_states, out_grad, cross_key, cross_value, cross_query, cross_out.T]
-    qb, da, ks, gq, vnT, gradT, mu, inv, edge, sidx = call(encode, "encode", 0, args, [M] * 3 + [V] * 2 + [A] * 12, P_OUT, (8, 160), P_SCRATCH, P_TABLES.values())
+    qb, da, ks, mu, inv, gq, vnT, gradT, edge, sidx = call(encode, "encode", 0, args, [M] * 3 + [V] * 2 + [A] * 12, P_OUT, P_FAR, (8, 160), P_SCRATCH, P_TABLES.values())
     args = [edge, sidx, qb, da, ks, mu, inv, gq, vnT, gradT, video_states, out_grad]
-    outs = call(attend, "attend", 1, args, [M] * 2 + [V] * 5 + [A] * 5, Q_OUT, (), Q_SCRATCH, ())
+    outs = call(attend, "attend", 1, args, [M] * 2 + [V] * 5 + [A] * 5, Q_OUT, {}, (), Q_SCRATCH, ())
     updated, igrad, qgrad, ograd, kgrad, vgrad = pl.pallas_call(
         hand_over,
         out_shape=tuple(jax.ShapeDtypeStruct(s, d) for s, d in Q_OUT.values()),
         in_specs=[pl.BlockSpec(memory_space=A)] * 6,
         out_specs=(pl.BlockSpec(memory_space=A),) * 6,
-        scratch_shapes=[DMA((6,))],
+        scratch_shapes=[V(s, d) for s, d in Q_OUT.values()] + [DMA((12,))],
         name="hand_over",
     )(*outs)
     return updated, igrad, qgrad, ograd.T, kgrad[None], vgrad[None]

time: 167 us -> 130 us (0.78)
  Pallas kernels: 166 us -> 129 us
    pallas_call x1, Pallas kernels: 39.9 us -> 2.13 us  [local(): pl.pallas_call(hand_over, out_shape=tuple((jax.ShapeDtypeStruct(s, d) for...]
where the time goes in v4:
time: 130 us
  Pallas kernels  129 us (99%)
    pallas_call x2, Pallas kernels, call(): pl.pallas_call(kernel, out_shape=tuple((jax.ShapeDtypeStruct(s, d) for s,...  127 us

profile of v4, /device:TPU:1, one launch (start us, length us, event | category | flops | bytes accessed | tf_op | source)
XLA Modules:
  0.0 129.6 jit_solution(17975397160919382042)
XLA Ops:
  0.6 65.1 %encode.1 = (bf16[256,384]{1,0:T(8,128)(2,1)}, bf16[256,384]{1,0:T(8,128)(2,1)}, bf16[2,384,384]{2,1,0:T(8,128)(2,1)}, f32[256,1]{1,0:T(8,128)}, f32[256,1]{1,0:...) custom-call(s32[32]{0:T(128)} %refs_0_.1, ...), custom_call_target="tpu_custom_call" | custom-call | tf_op jit(solution)/shard_map/encode/pallas_call | solution.py:837
  65.7 61.5 %attend.1 = (bf16[256,768]{1,0:T(8,128)(2,1)}, bf16[256,768]{1,0:T(8,128)(2,1)}, f32[96,384]{1,0:T(8,128)}, f32[96,384]{1,0:T(8,128)}, bf16[128,384]{1,0:T(8,128)(2,1)}, /*index=5*/bf16[128,384]{1,0:T(8,128)(2,1)}) custom-call(s32[8]{0:T(128)} %get-tuple-element.28.refs_0_, s32[160]{0:T(256)} %get-tuple-element.29.refs_1_, ...), custom_call_target="tpu_custom_call" | custom-call | tf_op jit(solution)/shard_map/attend/pallas_call | solution.py:837
  127.3 2.1 %hand_over.1 = (bf16[256,768]{1,0:T(8,128)(2,1)}, bf16[256,768]{1,0:T(8,128)(2,1)}, f32[96,384]{1,0:T(8,128)}, f32[96,384]{1,0:T(8,128)}, bf16[128,384]{1,0:T(8,128)(2,1)}, /*index=5*/bf16[128,384]{1,0:T(8,128)(2,1)}) custom-call(bf16[256,768]{1,0:T(8,128)(2,1)} %get-tuple-element.38.refs_0_, bf16[256,768]{1,0:T(8,128)(2,1)} %get-tuple-element.39.refs_1_, ...), custom_call_target="tpu_custom_call" | custom-call | tf_op jit(solution)/shard_map/hand_over/pallas_call | solution.py:850

commit v5 on v4

--- a/solution.py
+++ b/solution.py
@@ -548,9 +548,9 @@
     sb[4]()
     sb[5]()
     T.mid()
-    fill_tables(r)
     sa[6]()
     sb[6]()
+    fill_tables(r)
     T.end()
 
     @pl.loop(0, 8)
@@ -746,7 +746,12 @@
     s2[1]()
     s2[2]()
     s1[8]()
-    s2[3]()
+    for i in (3, 4):
+        s2[i]()
+    for i in (9, 10):
+        s1[i]()
+    for i in (5, 6, 7):
+        s2[i]()
     r.RG[pl.ds(96, 3)] = jnp.zeros((3, 8, 384), BF)
     r.RG[pl.ds(3 * f, 3)] = r.T[f]
     wait_bytes(r.RG.at[pl.ds(0, 93)], r.asem.at[4], r.asem.at[5], partner)
@@ -763,10 +768,7 @@
         to = (f + j) % 32
         pltpu.make_async_remote_copy(src_ref=r.CG.at[to], dst_ref=r.KV.at[f], send_sem=r.asem.at[6], recv_sem=r.asem.at[7], device_id={"grp": g, "fsdp": to}, device_id_type=MESH).start()
     r.KV[f] = r.CG[f]
-    for i in (9, 10):
-        s1[i]()
-    for i in (4, 5):
-        s2[i]()
+    s2[8]()
     O.end()
     loads["vid"].wait()
     loads["grad"].wait()
@@ -776,8 +778,6 @@
     def _(i):
         rows = pl.ds(i * 16, 16)
         r.updated[rows] = (r.vid[rows, cols].astype(F32) + O.total(rows)).astype(BF)
-    s2[6]()
-    s2[7]()
     N.end()
 
     def video_hat(rows):
@@ -794,7 +794,7 @@
     grp = [{"grp": (g + j) % 4, "fsdp": f} for j in range(1, 4)]
     for j in range(1, 4):
         L.send(r.stat.at[g], r.stat.at[g], ("st", j), grp[j - 1])
-    for i in (8, 9, 10):
+    for i in (9, 10):
         s2[i]()
     r.ograd[...] = S1.result()
     for j in range(1, 4):

time: 130 us -> 129 us (level)
  no operation moved by 1% of the time
where the time goes in v5:
time: 129 us
  Pallas kernels  128 us (99%)
    pallas_call x2, Pallas kernels, call(): pl.pallas_call(kernel, out_shape=tuple((jax.ShapeDtypeStruct(s, d) for s,...  126 us

profile of v5, /device:TPU:1, one launch (start us, length us, event | category | flops | bytes accessed | tf_op | source)
XLA Modules:
  0.0 129.2 jit_solution(3886595668051796373)
XLA Ops:
  0.6 65.1 %encode.1 = (bf16[256,384]{1,0:T(8,128)(2,1)}, bf16[256,384]{1,0:T(8,128)(2,1)}, bf16[2,384,384]{2,1,0:T(8,128)(2,1)}, f32[256,1]{1,0:T(8,128)}, f32[256,1]{1,0:...) custom-call(s32[32]{0:T(128)} %refs_0_.1, ...), custom_call_target="tpu_custom_call" | custom-call | tf_op jit(solution)/shard_map/encode/pallas_call | solution.py:837
  65.7 61.2 %attend.1 = (bf16[256,768]{1,0:T(8,128)(2,1)}, bf16[256,768]{1,0:T(8,128)(2,1)}, f32[96,384]{1,0:T(8,128)}, f32[96,384]{1,0:T(8,128)}, bf16[128,384]{1,0:T(8,128)(2,1)}, /*index=5*/bf16[128,384]{1,0:T(8,128)(2,1)}) custom-call(s32[8]{0:T(128)} %get-tuple-element.28.refs_0_, s32[160]{0:T(256)} %get-tuple-element.29.refs_1_, ...), custom_call_target="tpu_custom_call" | custom-call | tf_op jit(solution)/shard_map/attend/pallas_call | solution.py:837
  126.9 2.1 %hand_over.1 = (bf16[256,768]{1,0:T(8,128)(2,1)}, bf16[256,768]{1,0:T(8,128)(2,1)}, f32[96,384]{1,0:T(8,128)}, f32[96,384]{1,0:T(8,128)}, bf16[128,384]{1,0:T(8,128)(2,1)}, /*index=5*/bf16[128,384]{1,0:T(8,128)(2,1)}) custom-call(bf16[256,768]{1,0:T(8,128)(2,1)} %get-tuple-element.38.refs_0_, bf16[256,768]{1,0:T(8,128)(2,1)} %get-tuple-element.39.refs_1_, ...), custom_call_target="tpu_custom_call" | custom-call | tf_op jit(solution)/shard_map/hand_over/pallas_call | solution.py:850

commit v6 on v5

--- a/solution.py
+++ b/solution.py
@@ -119,11 +119,16 @@
         m = self.me
         self.L.sent(self.G.at[pl.ds(0, 31)], self.name, (self.name, "x"), {"grp": m["g"], "fsdp": m["f"] + 1 - 2 * m["x"]})
 
-def barrier(me, devs):
+def greet(devs):
     b = pltpu.get_barrier_semaphore()
     for d in devs:
         pl.semaphore_signal(b, inc=1, device_id=d, device_id_type=MESH)
-    pl.semaphore_wait(b, len(devs))
+    return len(devs)
+
+
+def meet(count):
+    pl.semaphore_wait(pltpu.get_barrier_semaphore(), count)
+
 
 def neighbours(me):
     m = me
@@ -451,6 +456,8 @@
     r = named(refs, P_IN + list(P_OUT) + [n + "_o" for n in P_FAR] + ["edge", "sidx"] + list(P_FAR) + list(P_SCRATCH) + list(P_TABLES) + ["sems", "lsem", "asem"])
     me = place()
     f, g, core, hi = me["f"], me["g"], me["core"], me["hi"]
+    fs = [{"grp": g, "fsdp": (f + j) % 32} for j in range(1, 32)]
+    count = greet(fs + [{"grp": (g + j) % 4, "fsdp": f // 2 * 2 + x} for j in range(1, 4) for x in range(2)])
     L = Links(r.sems)
     loads = {}
 
@@ -475,8 +482,7 @@
     load("grad", r.grad_h, r.grad)
 
     others = eight_others(me)
-    fs = [{"grp": g, "fsdp": (f + j) % 32} for j in range(1, 32)]
-    barrier(me, fs + [{"grp": (g + j) % 4, "fsdp": f // 2 * 2 + x} for j in range(1, 4) for x in range(2)])
+    meet(count)
 
     A, B = Gather(L, me, "w", r.gw, 128), Gather(L, me, "q", r.gq, 192)
     sa, sb = A.stages(r.kv.at[me["x"]]), B.stages(r.qo)
@@ -660,13 +666,13 @@
     r = named(refs, Q_IN + list(Q_OUT) + list(Q_SCRATCH) + ["sems", "lsem", "asem"])
     me = place()
     f, g, core, hi = me["f"], me["g"], me["core"], me["hi"]
+    count = greet([{"grp": g, "fsdp": (f + j) % 32} for j in range(1, 32)] + [{"grp": (g + j) % 4, "fsdp": f} for j in range(1, 4)])
     L = Links(r.sems)
     partner = {"grp": g, "fsdp": (f + 1) % 32}
     loads = {}
     for i, n in enumerate(("gradT", "gq", "vnT", "vid", "grad")):
         loads[n] = pltpu.make_async_copy(getattr(r, n + "_h"), getattr(r, n), r.lsem.at[i])
         loads[n].start()
-    barrier(me, [{"grp": g, "fsdp": (f + j) % 32} for j in range(1, 32)] + [{"grp": (g + j) % 4, "fsdp": f} for j in range(1, 4)])
     position = lax.broadcasted_iota(jnp.int32, (256, 128), 0) + f * 256
     slot = (position >= r.edge[0]).astype(jnp.int32) + (position >= r.edge[1]).astype(jnp.int32)
     token_len = jnp.where(slot == 0, r.edge[2], jnp.where(slot == 1, r.edge[3], r.edge[4]))
@@ -699,6 +705,7 @@
     S1 = Scatter(L, me, "d1", r.Dw, r.ra1, r.rb1, r.rx1)
     S2 = Scatter(L, me, "d2", r.Dq, r.ra2, r.rb2, r.rx2)
     s1, s2 = S1.stages(), S2.stages()
+    meet(count)
     s1[0]()
     loads["gq"].wait()
     O = TwoStep(L, me, "o", r.op, r.o0, r.o1, r.o2, r.o3)

time: 129 us -> 126 us (0.977)
  Pallas kernels: 128 us -> 125 us
    pallas_call x2, Pallas kernels: 126 us -> 123 us  [call(): pl.pallas_call(kernel, out_shape=tuple((jax.ShapeDtypeStruct(s, d) for s,...]
where the time goes in v6:
time: 126 us
  Pallas kernels  125 us (99%)
    pallas_call x2, Pallas kernels, call(): pl.pallas_call(kernel, out_shape=tuple((jax.ShapeDtypeStruct(s, d) for s,...  123 us

profile of v6, /device:TPU:1, one launch (start us, length us, event | category | flops | bytes accessed | tf_op | source)
XLA Modules:
  0.0 125.6 jit_solution(13010394623083148514)
XLA Ops:
  0.6 65.0 %encode.1 = (bf16[256,384]{1,0:T(8,128)(2,1)}, bf16[256,384]{1,0:T(8,128)(2,1)}, bf16[2,384,384]{2,1,0:T(8,128)(2,1)}, f32[256,1]{1,0:T(8,128)}, f32[256,1]{1,0:...) custom-call(s32[32]{0:T(128)} %refs_0_.1, ...), custom_call_target="tpu_custom_call" | custom-call | tf_op jit(solution)/shard_map/encode/pallas_call | solution.py:844
  65.7 57.6 %attend.1 = (bf16[256,768]{1,0:T(8,128)(2,1)}, bf16[256,768]{1,0:T(8,128)(2,1)}, f32[96,384]{1,0:T(8,128)}, f32[96,384]{1,0:T(8,128)}, bf16[128,384]{1,0:T(8,128)(2,1)}, /*index=5*/bf16[128,384]{1,0:T(8,128)(2,1)}) custom-call(s32[8]{0:T(128)} %get-tuple-element.28.refs_0_, s32[160]{0:T(256)} %get-tuple-element.29.refs_1_, ...), custom_call_target="tpu_custom_call" | custom-call | tf_op jit(solution)/shard_map/attend/pallas_call | solution.py:844
  123.3 2.1 %hand_over.1 = (bf16[256,768]{1,0:T(8,128)(2,1)}, bf16[256,768]{1,0:T(8,128)(2,1)}, f32[96,384]{1,0:T(8,128)}, f32[96,384]{1,0:T(8,128)}, bf16[128,384]{1,0:T(8,128)(2,1)}, /*index=5*/bf16[128,384]{1,0:T(8,128)(2,1)}) custom-call(bf16[256,768]{1,0:T(8,128)(2,1)} %get-tuple-element.38.refs_0_, bf16[256,768]{1,0:T(8,128)(2,1)} %get-tuple-element.39.refs_1_, ...), custom_call_target="tpu_custom_call" | custom-call | tf_op jit(solution)/shard_map/hand_over/pallas_call | solution.py:857

commit v7 on v6

--- a/solution.py
+++ b/solution.py
@@ -710,10 +710,6 @@
     loads["gq"].wait()
     O = TwoStep(L, me, "o", r.op, r.o0, r.o1, r.o2, r.o3)
     N = TwoStep(L, me, "n", r.dn, r.n0, r.n1, r.n2, r.n3)
-    for j, s in enumerate(O.order()):
-        r.op[s] = dot(r.att[...], r.gq[pl.ds(s * 8, 8), 96:192].reshape(768, 384), 1, 1).astype(BF)
-        if j < 2:
-            O.start(j)
     s1[1]()
 
     for h in range(3):
@@ -724,10 +720,13 @@
         ms = placed(ds)
         r.ms[h] = ms
         r.dq[:, cols] = dot(ms, r.ks[0, :, cols], 1, 0).astype(BF)
-    O.mid()
     loads["vnT"].wait()
     weight_grad(r.Dq, r.vnT, r.dq)
     s2[0]()
+    for j, s in enumerate(O.order()):
+        r.op[s] = dot(r.att[...], r.gq[pl.ds(s * 8, 8), 96:192].reshape(768, 384), 1, 1).astype(BF)
+        if j < 2:
+            O.start(j)
     s1[2]()
     s1[3]()
     for j, s in enumerate(N.order()):
@@ -747,6 +746,7 @@
     def _(j):
         to = (f + j) % 32
         pltpu.make_async_remote_copy(src_ref=r.T.at[to], dst_ref=r.RG.at[pl.ds(3 * f, 3)], send_sem=r.asem.at[4], recv_sem=r.asem.at[5], device_id={"grp": g, "fsdp": to}, device_id_type=MESH).start()
+    O.mid()
     N.mid()
     for i in range(4, 8):
         s1[i]()

time: 126 us -> 126 us (level)
  no operation moved by 1% of the time
where the time goes in v7:
time: 126 us
  Pallas kernels  125 us (99%)
    pallas_call x2, Pallas kernels, call(): pl.pallas_call(kernel, out_shape=tuple((jax.ShapeDtypeStruct(s, d) for s,...  123 us

profile of v7, /device:TPU:1, one launch (start us, length us, event | category | flops | bytes accessed | tf_op | source)
XLA Modules:
  0.0 125.5 jit_solution(15209694503155387444)
XLA Ops:
  0.6 65.0 %encode.1 = (bf16[256,384]{1,0:T(8,128)(2,1)}, bf16[256,384]{1,0:T(8,128)(2,1)}, bf16[2,384,384]{2,1,0:T(8,128)(2,1)}, f32[256,1]{1,0:T(8,128)}, f32[256,1]{1,0:...) custom-call(s32[32]{0:T(128)} %refs_0_.1, ...), custom_call_target="tpu_custom_call" | custom-call | tf_op jit(solution)/shard_map/encode/pallas_call | solution.py:844
  65.7 57.6 %attend.1 = (bf16[256,768]{1,0:T(8,128)(2,1)}, bf16[256,768]{1,0:T(8,128)(2,1)}, f32[96,384]{1,0:T(8,128)}, f32[96,384]{1,0:T(8,128)}, bf16[128,384]{1,0:T(8,128)(2,1)}, /*index=5*/bf16[128,384]{1,0:T(8,128)(2,1)}) custom-call(s32[8]{0:T(128)} %get-tuple-element.28.refs_0_, s32[160]{0:T(256)} %get-tuple-element.29.refs_1_, ...), custom_call_target="tpu_custom_call" | custom-call | tf_op jit(solution)/shard_map/attend/pallas_call | solution.py:844
  123.2 2.1 %hand_over.1 = (bf16[256,768]{1,0:T(8,128)(2,1)}, bf16[256,768]{1,0:T(8,128)(2,1)}, f32[96,384]{1,0:T(8,128)}, f32[96,384]{1,0:T(8,128)}, bf16[128,384]{1,0:T(8,128)(2,1)}, /*index=5*/bf16[128,384]{1,0:T(8,128)(2,1)}) custom-call(bf16[256,768]{1,0:T(8,128)(2,1)} %get-tuple-element.38.refs_0_, bf16[256,768]{1,0:T(8,128)(2,1)} %get-tuple-element.39.refs_1_, ...), custom_call_target="tpu_custom_call" | custom-call | tf_op jit(solution)/shard_map/hand_over/pallas_call | solution.py:857
